TPU v7x, 32 devices: a whole 2x2x4 slice. The times are simulated.
32 devices in a mesh: wide: 8 (over z, x), narrow: 4 (over y, core).
Axes of the slice: x: 2, y: 2, z: 4, core: 2. Of those that a mesh axis runs over, the one named last changes fastest.
Arguments:
- tokens_in: bfloat16 [1024, 2560], P('wide', 'narrow'), may hold values from -6 to 6
- norm_gain: bfloat16 [2560], replicated, may hold values from 0.099609375 to 1.8984375
- query_weight: bfloat16 [2560, 2560], P('wide', 'narrow'), may hold values from -0.25 to 0.25
- key_weight: bfloat16 [2560, 640], P('wide', 'narrow'), may hold values from -0.125 to 0.125
- value_weight: bfloat16 [2560, 640], P('wide', 'narrow'), may hold values from -0.5 to 0.5
- out_weight: bfloat16 [2560, 2560], P('wide', 'narrow'), may hold values from -0.125 to 0.125
- cache_keys: bfloat16 [640, 8192], P('narrow', 'wide'), may hold values from -64 to 64
- cache_values: bfloat16 [640, 8192], P('narrow', 'wide'), may hold values from -24 to 24
- cached_len: int32 [2], replicated, may hold values from 1 to 4096, as said below
- append_slot: int32 [2], replicated, may hold values from 0 to 4095
- shard_owner: int32 [2], replicated, may hold values from 0 to 3
Outputs:
- attention_update: bfloat16 [1024, 2560], P('wide', 'narrow')
- appended_keys: bfloat16 [640, 8192], P('narrow', 'wide')
- appended_values: bfloat16 [640, 8192], P('narrow', 'wide')
Inputs may be any that keep to these rules, and one draw needn't show every extreme that they name: `cached_len`: each request's number of cached keys; some request holds 4096.
All inputs are finite; a program needn't handle non-finite values.
Results may differ from a plain program's by a relative error of at most 0.012.
The roundings to bfloat16 on the way count: a program that leaves them out, or rounds other values in their place, can miss the bound.
Values may be sent and summed in bfloat16 or wider, within the bound.
No kernel may reach another device: no remote copies, remote signals or barrier semaphores. Data moves between devices by JAX's collectives and lax.ppermute only.
A program may use at most 64 MiB of HBM per device.

v0:
```python
import math

import jax
import jax.numpy as jnp
from jax import lax
from jax.sharding import PartitionSpec as P

HEAD_DIM = 80
WIN = 4096
GROUP_BITS = 2
GROUP = 4


EPSILON = 1e-05
ROPE_BASE = 10000.0
LOWEST = -1e30


def from_partner(block, axis, bit):
    count = lax.axis_size(axis)
    route = []
    for low in range(count):
        high = low | 1 << bit
        if high != low and high < count:
            route += [(low, high), (high, low)]
    return lax.ppermute(block, axis, route)


def rms_normed(rows_in, gain):
    values = rows_in.astype(jnp.float32)
    scaling = lax.rsqrt(jnp.mean(values * values, axis=-1, keepdims=True) + EPSILON)
    return (values * scaling * gain.astype(jnp.float32)).astype(jnp.bfloat16)


def rotate(values, positions):
    half_dim = values.shape[-1] // 2
    inverse = ROPE_BASE ** (-(jnp.arange(half_dim, dtype=jnp.float32) * (2.0 / values.shape[-1])))
    angles = positions.astype(jnp.float32)[:, None] * inverse[None, :]
    cos_part = jnp.cos(angles)[:, None, :]
    sin_part = jnp.sin(angles)[:, None, :]
    lower = values[..., :half_dim]
    higher = values[..., half_dim:]
    return jnp.concatenate(
        [lower * cos_part - higher * sin_part, higher * cos_part + lower * sin_part], axis=-1
    )


def ordered(mine, other, upper, along):
    first_half = jnp.where(upper, other, mine)
    second_half = jnp.where(upper, mine, other)
    return jnp.concatenate([first_half, second_half], axis=along)


def empty_state(row_count, groups, repeats):
    return (
        jnp.zeros((row_count, groups, repeats, HEAD_DIM), jnp.float32),
        jnp.full((row_count, groups, repeats), LOWEST, jnp.float32),
        jnp.zeros((row_count, groups, repeats), jnp.float32),
    )


def fold_keys(state, queries, query_pos, keys, values, key_pos, key_ok, widest):
    key_count = keys.shape[1]
    groups = queries.shape[1]
    block = math.gcd(key_count, widest)
    keys_split = keys.reshape(groups, HEAD_DIM, key_count)
    values_split = values.reshape(groups, HEAD_DIM, key_count)
    scale = HEAD_DIM ** (-0.5)

    def step(index, carry):
        accum, top_old, sum_old = carry
        start = index * block
        block_keys = lax.dynamic_slice_in_dim(keys_split, start, block, 2)
        block_values = lax.dynamic_slice_in_dim(values_split, start, block, 2)
        block_pos = lax.dynamic_slice_in_dim(key_pos, start, block, 0)
        block_ok = lax.dynamic_slice_in_dim(key_ok, start, block, 0)
        scores = (
            jnp.einsum("tgrd,gdk->tgrk", queries, block_keys, preferred_element_type=jnp.float32)
            * scale
        )
        allowed = (
            block_ok[None, :]
            & (block_pos[None, :] <= query_pos[:, None])
            & (query_pos[:, None] - block_pos[None, :] < WIN)
        )
        allowed = allowed[:, None, None, :]
        top_new = jnp.maximum(top_old, jnp.max(jnp.where(allowed, scores, LOWEST), axis=-1))
        weights = jnp.where(allowed, jnp.exp(scores - top_new[..., None]), 0.0)
        rescale = jnp.exp(top_old - top_new)
        sum_new = sum_old * rescale + jnp.sum(weights, axis=-1)
        mixed = jnp.einsum(
            "tgrk,gdk->tgrd",
            weights.astype(jnp.bfloat16),
            block_values,
            preferred_element_type=jnp.float32,
        )
        return (accum * rescale[..., None] + mixed, top_new, sum_new)

    return lax.fori_loop(0, key_count // block, step, state)


def shards(
    tokens_in,
    norm_gain,
    query_weight,
    key_weight,
    value_weight,
    out_weight,
    cache_keys,
    cache_values,
    cached_len,
    append_slot,
    shard_owner,
):
    whole = lax.all_gather(tokens_in, "narrow", axis=1, tiled=True)
    normed = rms_normed(whole, norm_gain)
    tok_rows = whole.shape[0]
    query_width = query_weight.shape[1]
    kv_width = key_weight.shape[1]
    local_heads = query_width // HEAD_DIM
    local_groups = kv_width // HEAD_DIM
    repeats = local_heads // local_groups
    columns = normed
    query_sum = jnp.dot(
        columns,
        lax.all_gather(query_weight, "wide", axis=0, tiled=True),
        preferred_element_type=jnp.float32,
    )
    key_sum = jnp.dot(
        columns,
        lax.all_gather(key_weight, "wide", axis=0, tiled=True),
        preferred_element_type=jnp.float32,
    )
    value_sum = jnp.dot(
        columns,
        lax.all_gather(value_weight, "wide", axis=0, tiled=True),
        preferred_element_type=jnp.float32,
    )
    position = lax.axis_index("wide")
    request = position // GROUP
    place = position % GROUP
    length = cached_len[request]
    offset = append_slot[request]
    owner = shard_owner[request]
    query_pos = length + place * tok_rows + jnp.arange(tok_rows, dtype=jnp.int32)
    queries = rotate(query_sum.reshape(tok_rows, local_heads, HEAD_DIM), query_pos).astype(
        jnp.bfloat16
    )
    queries = queries.reshape(tok_rows, local_groups, repeats, HEAD_DIM)
    new_keys = (
        rotate(key_sum.reshape(tok_rows, local_groups, HEAD_DIM), query_pos)
        .astype(jnp.bfloat16)
        .reshape(tok_rows, kv_width)
    )
    new_values = value_sum.astype(jnp.bfloat16)
    shard_rows = cache_keys.shape[1]
    within = jnp.arange(shard_rows, dtype=jnp.int32)
    cycle_mine = (place - owner) % GROUP * shard_rows + within
    old_keys, old_values = (cache_keys, cache_values)
    for bit in range(GROUP_BITS):
        upper = place // 2**bit % 2 == 1
        other_keys, other_values, other_old_keys, other_old_values = from_partner(
            (new_keys, new_values, old_keys, old_values), "wide", bit
        )
        new_keys = ordered(new_keys, other_keys, upper, 0)
        new_values = ordered(new_values, other_values, upper, 0)
        old_keys = ordered(old_keys, other_old_keys, upper, 1)
        old_values = ordered(old_values, other_old_values, upper, 1)
    slot_index = jnp.arange(old_keys.shape[1], dtype=jnp.int32)
    cycle = (slot_index // shard_rows - owner) % GROUP * shard_rows + slot_index % shard_rows
    cached_pos = (cycle - offset + length) % WIN
    state = fold_keys(
        empty_state(tok_rows, local_groups, repeats),
        queries,
        query_pos,
        old_keys,
        old_values,
        cached_pos,
        cached_pos < length,
        512,
    )
    key_cols = new_keys.T
    value_cols = new_values.T
    new_count = key_cols.shape[1]
    new_pos = length + jnp.arange(new_count, dtype=jnp.int32)
    state = fold_keys(
        state,
        queries,
        query_pos,
        key_cols,
        value_cols,
        new_pos,
        jnp.ones((new_count,), dtype=bool),
        512,
    )
    accum, top_score, total = state
    attended = (accum / total[..., None]).astype(jnp.bfloat16).reshape(tok_rows, query_width)
    all_heads = lax.all_gather(attended, "narrow", axis=1, tiled=True)
    columns = all_heads
    update = jnp.dot(
        columns,
        lax.all_gather(out_weight, "wide", axis=0, tiled=True),
        preferred_element_type=jnp.float32,
    ).astype(jnp.bfloat16)
    new_index = (cycle_mine - offset) % WIN
    written = new_index < new_count
    take_rows = jnp.minimum(new_index, new_count - 1)
    put_keys = jnp.where(written[None, :], jnp.take(key_cols, take_rows, axis=1), cache_keys)
    put_values = jnp.where(written[None, :], jnp.take(value_cols, take_rows, axis=1), cache_values)
    return (update, put_keys, put_values)


def solution(mesh):
    in_specs = (
        P("wide", "narrow"),
        P(),
        P("wide", "narrow"),
        P("wide", "narrow"),
        P("wide", "narrow"),
        P("wide", "narrow"),
        P("narrow", "wide"),
        P("narrow", "wide"),
        P(),
        P(),
        P(),
    )
    out_specs = (P("wide", "narrow"), P("narrow", "wide"), P("narrow", "wide"))
    return jax.shard_map(shards, mesh=mesh, in_specs=in_specs, out_specs=out_specs, check_vma=False)
```

profile of v0, /device:TPU:0, one launch (start us, length us, event | category | flops | bytes accessed | tf_op | source)
XLA Modules:
  0.0 243.9 jit_solution(6396453036304383241)
XLA Ops:
  8.7 36.8 %all-gather = bf16[8,320,160]{1,2,0:T(8,128)(2,1)S(1)} all-gather(bf16[1,320,160]{1,2,0:T(8,128)(2,1)} %bitcast.132), channel_id=1, replica_groups=mesh['wide'=8,'narrow'=4] {'wide'}, dimensions={0}, use_global_device_ids=true | all-gather | bytes 921600 | tf_op jit(solution)/shard_map/all_gather | solution.py:131
  47.8 8.0 %all_gather.18 = bf16[128,2560]{1,0:T(8,128)(2,1)S(1)} all-gather(bf16[128,640]{1,0:T(8,128)(2,1)S(1)} %copy-done.9), channel_id=1, replica_groups=mesh['wide'=8,'narrow'=4] {'narrow'}, dimensions={1}, use_global_device_ids=true | all-gather | bytes 819200 | tf_op jit(solution)/shard_map/all_gather | solution.py:115
  57.4 35.7 %all-gather.1 = bf16[8,320,160]{1,2,0:T(8,128)(2,1)S(1)} all-gather(bf16[1,320,160]{1,2,0:T(8,128)(2,1)S(1)} %bitcast.133), channel_id=1, replica_groups=mesh['wide'=8,'narrow'=4] {'wide'}, dimensions={0}, use_global_device_ids=true | all-gather | bytes 921600 | tf_op jit(solution)/shard_map/all_gather | solution.py:136
  94.7 2.0 collective-permute-start
  98.7 2.6 %add_select_fusion = s32[4096]{0:T(1024)} fusion(s32[]{:T(128)} %bitcast.2, s32[]{:T(128)} %bitcast.1, s32[]{:T(128)} %bitcast), kind=kLoop, calls=%fused_computation.96 | loop fusion | flops 159744 | bytes 16396 | tf_op jit(solution)/shard_map/jit(remainder)/select_n | solution.py:171
  101.3 2.6 %broadcast_compare_fusion = pred[4096]{0:T(1024)(128)(4,1)} fusion(s32[]{:T(128)} %bitcast.2, s32[]{:T(128)} %bitcast.1, s32[]{:T(128)} %bitcast), kind=kLoop, calls=%fused_computation.114 | loop fusion | flops 163840 | bytes 4108 | tf_op jit(solution)/shard_map/lt | solution.py:179
  108.4 2.0 collective-permute-start.7
  110.4 1.8 collective-permute-done.5
  113.1 3.6 %collective-permute-done.7 = bf16[256,160]{0,1:T(8,128)(2,1)S(1)} collective-permute-done((bf16[256,160]{0,1:T(8,128)(2,1)}, bf16[256,160]{0,1:T(8,128)(2,1)S(1)}, u32[]{:S(2)}, u32[]{:S(2)}) %collective-permute-start.7) | collective-permute-done | bytes 81952 | tf_op jit(solution)/shard_map/ppermute | solution.py:26
  122.0 5.0 %gather_fusion = bf16[1024,160]{1,0:T(8,128)(2,1)} fusion(bf16[160,512]{0,1:T(8,128)(2,1)S(1)} %copy.42, s32[1024]{0:T(1024)S(1)} %fusion.54), kind=kCustom, calls=%fused_computation.clone | custom fusion | bytes 659456 | tf_op jit(solution)/shard_map/jit(_take)/gather | solution.py:208
  126.9 4.9 %gather_fusion.1 = bf16[1024,160]{1,0:T(8,128)(2,1)} fusion(bf16[160,512]{0,1:T(8,128)(2,1)S(1)} %copy.44, s32[1024]{0:T(1024)S(1)} %fusion.54), kind=kCustom, calls=%fused_computation.1.clone | custom fusion | bytes 659456 | tf_op jit(solution)/shard_map/jit(_take)/gather | solution.py:209
  131.9 2.9 %bitcast_select_fusion.2 = (bf16[160,1024]{0,1:T(8,128)(2,1)S(1)}, bf16[160,1024]{0,1:T(8,128)(2,1)}) fusion(bf16[160,1024]{0,1:T(8,128)(2,1)S(1)} %copy.45, bf16[1024,160]{1,0:T(8,128)(2,1)} %gather_fusion.1, pred[1024]{0:T(1024)(128)(4,1)S(1)} %get-tuple-element.313, pred[1024]{0:T(1024)(128)(4,1)} %get-tuple-element.314, bf16[160,1024]{0,1:T(8,128)(2,1)S(1)} %copy.43, ...), kind=kLoop, calls=%fused_computation.61 | loop fusion | flops 655360 | bytes 1968128 | tf_op jit(solution)/shard_map/jit(_where)/select_n | solution.py:209
  134.8 1.9 copy.46
  137.7 1.6 collective-permute-start.1
  139.3 3.3 %collective-permute-done.3 = bf16[160,2048]{1,0:T(8,128)(2,1)} collective-permute-done((bf16[160,2048]{1,0:T(8,128)(2,1)}, bf16[160,2048]{1,0:T(8,128)(2,1)}, u32[]{:S(2)}, u32[]{:S(2)}) %collective-permute-start.3) | collective-permute-done | bytes 655392 | tf_op jit(solution)/shard_map/ppermute | solution.py:26
  145.2 33.9 %collective-permute-done.1 = bf16[160,2048]{1,0:T(8,128)(2,1)S(1)} collective-permute-done((bf16[160,2048]{1,0:T(8,128)(2,1)S(1)}, bf16[160,2048]{1,0:T(8,128)(2,1)S(1)}, u32[]{:S(2)}, u32[]{:S(2)}) %collective-permute-start.1) | collective-permute-done | bytes 655392 | tf_op jit(solution)/shard_map/ppermute | solution.py:26
  180.6 3.4 %fusion.64 = f32[128,640]{0,1:T(8,128)S(1)} fusion(bf16[2560,640]{1,0:T(8,128)(2,1)} %all-gather.5.cloned.1.call-done, bf16[128,2560]{1,0:T(8,128)(2,1)S(1)} %all_gather.18, f32[2560]{0:T(1024)S(1)} %copy-done.13, f32[128]{0:T(128)S(1)} %copy-done.15), kind=kOutput, calls=%fused_computation.135 | convolution fusion | flops 420741120 | bytes 4270592 | tf_op jit(solution)/shard_map/dot_general | solution.py:124
  184.1 41.1 %while.5 = (s32[]{:T(128)}, f32[128,2,4,80]{0,3,2,1:T(8,128)S(1)}, f32[128,2,4]{0,2,1:T(4,128)S(1)}, f32[128,2,4]{0,2,1:T(4,128)S(1)}, pred[4096]{0:T(1024)(128)...) while((s32[]{:T(128)}, f32[128,2,4,80]{0,3,2,1:T(8,128)S(1)}, ...), condition=%wide.region_4.5_spmd.clone, body=%wide.region_1.4_spmd.clone.sunk | while | flops 174118016 | bytes 7774931 | solution.py:99
  187.9 1.5 fusion.89
  198.1 1.5 fusion.89
  203.2 1.5 fusion.89
  223.8 1.5 fusion.89
  226.9 6.9 %all_gather.22 = bf16[128,2560]{0,1:T(8,128)(2,1)S(1)} all-gather(bf16[128,640]{0,1:T(8,128)(2,1)S(1)} %bitcast.130), channel_id=1, replica_groups=mesh['wide'=8,'narrow'=4] {'narrow'}, dimensions={1}, use_global_device_ids=true | all-gather | bytes 819200 | tf_op jit(solution)/shard_map/all_gather | solution.py:198
  233.8 3.3 %convolution_convert_fusion = bf16[128,640]{1,0:T(8,128)(2,1)} fusion(bf16[128,2560]{0,1:T(8,128)(2,1)S(1)} %all_gather.22, bf16[2560,640]{1,0:T(8,128)(2,1)} %all-gather.7.cloned.1.call-done), kind=kOutput, calls=%fused_computation.50 | convolution fusion | flops 419512320 | bytes 4096000 | tf_op jit(solution)/shard_map/dot_general | solution.py:200
  (182 shorter events, 59.4 us)
Async XLA Ops:
  7.2 173.4 %all-gather.5.cloned.1.call-start = ((), (), s32[]{:S(2)}) async-start(), calls=%async_computation | async-start | bytes 3686400 | tf_op jit(solution)/shard_map/all_gather | solution.py:126
  7.9 225.9 %all-gather.7.cloned.1.call-start = ((), (), s32[]{:S(2)}) async-start(), calls=%async_computation.1 | async-start | bytes 3686400 | tf_op jit(solution)/shard_map/all_gather | solution.py:202
  8.7 85.5 %copy-start.12 = (f32[2560]{0:T(1024)}, f32[2560]{0:T(1024)S(1)}, u32[]{:S(2)}) copy-start(f32[2560]{0:T(1024)S(1)} %convert_element_type.45) | copy-start | bytes 30724
  45.5 2.3 copy-start.9
  46.4 10.9 %copy-start.11 = (bf16[320,160]{0,1:T(8,128)(2,1)S(1)}, bf16[320,160]{0,1:T(8,128)(2,1)}, u32[]{:S(2)}) copy-start(bf16[320,160]{0,1:T(8,128)(2,1)} %param.19) | copy-start | bytes 307204
  56.0 38.2 %copy-start.14 = (f32[128]{0:T(128)}, f32[128]{0:T(128)S(1)}, u32[]{:S(2)}) copy-start(f32[128]{0:T(128)S(1)} %add_rsqrt_fusion) | copy-start | bytes 1540
  56.6 51.0 %collective-permute-start.4 = (bf16[128,160]{0,1:T(8,128)(2,1)S(1)}, bf16[128,160]{0,1:T(8,128)(2,1)S(1)}, u32[]{:S(2)}, u32[]{:S(2)}) collective-permute-start(bf16[128,160]{0,1:T(8,128)(2,1)S(1)} %bitcast.128), channel_id=1, source_target_pairs={{0,4},{4,0},{8,12},{12,8},{16,20},{20,16},{24,28},{28,24},{1,5},{5... | collective-permute-start | bytes 122888 | tf_op jit(solution)/shard_map/ppermute | solution.py:26
  93.5 3.3 %copy-start = (bf16[160,1024]{1,0:T(8,128)(2,1)S(1)}, bf16[160,1024]{1,0:T(8,128)(2,1)}, u32[]{:S(2)}) copy-start(bf16[160,1024]{1,0:T(8,128)(2,1)} %param.22) | copy-start | bytes 983044
  93.5 3.4 %copy-start.17 = (s32[2]{0:T(128)S(1)}, s32[2]{0:T(128)}, u32[]{:S(2)}) copy-start(s32[2]{0:T(128)} %param.25) | copy-start | bytes 28
  93.5 4.6 %copy-start.18 = (s32[2]{0:T(128)S(1)}, s32[2]{0:T(128)}, u32[]{:S(2)}) copy-start(s32[2]{0:T(128)} %param.24) | copy-start | bytes 28
  94.6 13.0 %collective-permute-start.6 = (bf16[128,160]{0,1:T(8,128)(2,1)S(1)}, bf16[128,160]{0,1:T(8,128)(2,1)S(1)}, u32[]{:S(2)}, u32[]{:S(2)}) collective-permute-start(bf16[128,160]{0,1:T(8,128)(2,1)S(1)} %convolution_convert_fusion.1), channel_id=1, source_target_pairs={{0,4},{4,0},{8,12},{12,8},{16,20},{20,16},{24,28},{28,24},{1,5},{5... | collective-permute-start | bytes 122888 | tf_op jit(solution)/shard_map/ppermute | solution.py:26
  94.7 22.0 %collective-permute-start = (bf16[160,1024]{1,0:T(8,128)(2,1)S(1)}, bf16[160,1024]{1,0:T(8,128)(2,1)S(1)}, u32[]{:S(2)}, u32[]{:S(2)}) collective-permute-start(bf16[160,1024]{1,0:T(8,128)(2,1)S(1)} %copy-done.1), channel_id=1, source_target_pairs={{0,4},{4,0},{8,12},{12,8},{16,20},{20,16},{24,28},{28,24},{1,5},{5... | collective-permute-start | bytes 983048 | tf_op jit(solution)/shard_map/ppermute | solution.py:26
  96.7 20.7 %collective-permute-start.2 = (bf16[160,1024]{1,0:T(8,128)(2,1)S(1)}, bf16[160,1024]{1,0:T(8,128)(2,1)}, u32[]{:S(2)}, u32[]{:S(2)}) collective-permute-start(bf16[160,1024]{1,0:T(8,128)(2,1)S(1)} %copy-done), channel_id=1, source_target_pairs={{0,4},{4,0},{8,12},{12,8},{16,20},{20,16},{24,28},{28,24},{1,5},{5... | collective-permute-start | bytes 983048 | tf_op jit(solution)/shard_map/ppermute | solution.py:26
  107.7 4.5 %collective-permute-start.5 = (bf16[256,160]{0,1:T(8,128)(2,1)S(1)}, bf16[256,160]{0,1:T(8,128)(2,1)S(1)}, u32[]{:S(2)}, u32[]{:S(2)}) collective-permute-start(bf16[256,160]{0,1:T(8,128)(2,1)S(1)} %pad_maximum_fusion.7), channel_id=1, source_target_pairs={{0,8},{8,0},{4,12},{12,4},{16,24},{24,16},{20,28},{28,20},{1,9},{9... | collective-permute-start | bytes 245768 | tf_op jit(solution)/shard_map/ppermute | solution.py:26
  108.4 8.2 %collective-permute-start.7 = (bf16[256,160]{0,1:T(8,128)(2,1)}, bf16[256,160]{0,1:T(8,128)(2,1)S(1)}, u32[]{:S(2)}, u32[]{:S(2)}) collective-permute-start(bf16[256,160]{0,1:T(8,128)(2,1)} %pad_maximum_fusion.8), channel_id=1, source_target_pairs={{0,8},{8,0},{4,12},{12,4},{16,24},{24,16},{20,28},{28,20},{1,9},{9... | collective-permute-start | bytes 245768 | tf_op jit(solution)/shard_map/ppermute | solution.py:26
  119.7 22.9 %collective-permute-start.3 = (bf16[160,2048]{1,0:T(8,128)(2,1)}, bf16[160,2048]{1,0:T(8,128)(2,1)}, u32[]{:S(2)}, u32[]{:S(2)}) collective-permute-start(bf16[160,2048]{1,0:T(8,128)(2,1)} %pad_maximum_fusion.3), channel_id=1, source_target_pairs={{0,8},{8,0},{4,12},{12,4},{16,24},{24,16},{20,28},{28,20},{1,9},{9... | collective-permute-start | bytes 1966088 | tf_op jit(solution)/shard_map/ppermute | solution.py:26
  137.7 41.4 %collective-permute-start.1 = (bf16[160,2048]{1,0:T(8,128)(2,1)S(1)}, bf16[160,2048]{1,0:T(8,128)(2,1)S(1)}, u32[]{:S(2)}, u32[]{:S(2)}) collective-permute-start(bf16[160,2048]{1,0:T(8,128)(2,1)S(1)} %pad_maximum_fusion.2), channel_id=1, source_target_pairs={{0,8},{8,0},{4,12},{12,4},{16,24},{24,16},{20,28},{28,20},{1,9},{9... | collective-permute-start | bytes 1966088 | tf_op jit(solution)/shard_map/ppermute | solution.py:26
  145.2 35.4 %copy-start.13 = (f32[2560]{0:T(1024)S(1)}, f32[2560]{0:T(1024)}, u32[]{:S(2)}) copy-start(f32[2560]{0:T(1024)} %copy-done.12) | copy-start | bytes 30724
  145.2 35.4 %copy-start.15 = (f32[128]{0:T(128)S(1)}, f32[128]{0:T(128)}, u32[]{:S(2)}) copy-start(f32[128]{0:T(128)} %copy-done.14) | copy-start | bytes 1540
  180.6 3.4 %copy-start.6 = (f32[128,40]{0,1:T(8,128)S(1)}, f32[128,40]{0,1:T(8,128)}, u32[]{:S(2)}) copy-start(f32[128,40]{0,1:T(8,128)} %copy-done.5) | copy-start | bytes 61444
  180.6 3.4 %copy-start.8 = (f32[128,40]{0,1:T(8,128)S(1)}, f32[128,40]{0,1:T(8,128)}, u32[]{:S(2)}) copy-start(f32[128,40]{0,1:T(8,128)} %copy-done.7) | copy-start | bytes 61444
  180.6 3.5 %copy-start.19 = (f32[128,2,4,80]{0,3,2,1:T(8,128)S(1)}, f32[128,2,4,80]{0,3,2,1:T(8,128)}, u32[]{:S(2)}) copy-start(f32[128,2,4,80]{0,3,2,1:T(8,128)} %custom-call) | copy-start | bytes 983044
  184.1 41.2 %copy-start.2 = (bf16[512,160]{0,1:T(8,128)(2,1)S(1)}, bf16[512,160]{0,1:T(8,128)(2,1)}, u32[]{:S(2)}) copy-start(bf16[512,160]{0,1:T(8,128)(2,1)} %get-tuple-element.292) | copy-start | bytes 491524
  184.1 41.2 %copy-start.3 = (pred[128,512]{0,1:T(8,128)(4,1)S(1)}, pred[128,512]{0,1:T(8,128)(4,1)}, u32[]{:S(2)}) copy-start(pred[128,512]{0,1:T(8,128)(4,1)} %fusion.38) | copy-start | bytes 196612
  (6 other events, 6.5 us)
Sparse Core Ops, SparseCore 0:
  10.2 89.5 all-gather.4
  102.0 79.1 all-gather.6
where the time goes:
time: 246 us; the launch traced here: 244 us
  blocking collectives  87.4 us (36%)
  waiting for transfers between devices  43.3 us (18%)
  matrix products  31.9 us (13%)
  local copies, waits for them, and re-layouts  30.8 us (13%)
  other arithmetic  26.9 us (11%)
  between operations  15.9 us (6%)
  starting transfers between devices  7.14 us (3%)
    ppermute x8, waiting for transfers between devices, from_partner(): return lax.ppermute(block, axis, route)  42.6 us
    all_gather x1, blocking collectives, shards(): lax.all_gather(key_weight, 'wide', axis=0, tiled=True)  36.8 us
    all_gather x1, blocking collectives, shards(): lax.all_gather(value_weight, 'wide', axis=0, tiled=True)  35.7 us
    dot_general x9, matrix products, step(): jnp.einsum('tgrk,gdk->tgrd', weights.astype(jnp.bfloat16), block_values,...  12.2 us
    dot_general x9, matrix products, step(): jnp.einsum('tgrd,gdk->tgrk', queries, block_keys, preferred_element_type=...  12 us
    all_gather x1, blocking collectives, shards(): whole = lax.all_gather(tokens_in, 'narrow', axis=1, tiled=True)  7.98 us
    ppermute x8, starting transfers between devices, from_partner(): return lax.ppermute(block, axis, route)  7.06 us
    all_gather x1, blocking collectives, shards(): all_heads = lax.all_gather(attended, 'narrow', axis=1, tiled=True)  6.87 us
  transfers between devices with their start and end apart: 10, of which 4 were waited for; matrix products, arithmetic and copies ran while one was open for 35% of the time, Pallas kernels for 0%

commit v1 on v0

--- a/solution.py
+++ b/solution.py
@@ -1,8 +1,11 @@
+import functools
 import math
 
 import jax
 import jax.numpy as jnp
 from jax import lax
+from jax.experimental import pallas as pl
+from jax.experimental.pallas import tpu as pltpu
 from jax.sharding import PartitionSpec as P
 
 HEAD_DIM = 80
@@ -99,7 +102,7 @@
     return lax.fori_loop(0, key_count // block, step, state)
 
 
-def shards(
+def shards_any(
     tokens_in,
     norm_gain,
     query_weight,
@@ -210,6 +213,594 @@
     return (update, put_keys, put_values)
 
 
+F32 = jnp.float32
+BF16 = jnp.bfloat16
+MASKED = -1e30
+FLOOR = -1e29
+EXP2_SCALE = HEAD_DIM ** (-0.5) * math.log2(math.e)
+CHUNK = 512
+NEW = 512
+
+
+def send(block, to):
+    route = []
+    for z in range(4):
+        for x in range(2):
+            for y in range(2):
+                for c in range(2):
+                    there = to(z, x, y, c)
+                    if there is not None:
+                        tz, tx, ty, tc = there
+                        route.append(((2 * z + x) * 4 + 2 * y + c, (2 * tz + tx) * 4 + 2 * ty + tc))
+    return lax.ppermute(block, ("wide", "narrow"), route)
+
+
+def after(block, *earlier):
+    return lax.optimization_barrier((block, *earlier))[0]
+
+
+def call(kernel, outs, *args, scalars=0, scratch=(), flops=1):
+    specs = [pl.BlockSpec(memory_space=pltpu.SMEM)] * scalars
+    specs += [pl.BlockSpec(memory_space=pltpu.VMEM)] * (len(args) - scalars)
+    return pl.pallas_call(
+        kernel,
+        out_shape=outs,
+        in_specs=specs,
+        out_specs=jax.tree.map(lambda _: pl.BlockSpec(memory_space=pltpu.VMEM), outs),
+        scratch_shapes=scratch,
+        compiler_params=pltpu.CompilerParams(vmem_limit_bytes=40 * 1024 * 1024),
+        cost_estimate=pl.CostEstimate(flops=flops, bytes_accessed=1, transcendentals=0),
+    )(*args)
+
+
+def shaped(shape, kind=BF16):
+    return jax.ShapeDtypeStruct(shape, kind)
+
+
+def coordinates():
+    wide = lax.axis_index("wide")
+    narrow = lax.axis_index("narrow")
+    return wide >> 1, wide & 1, narrow >> 1, narrow & 1
+
+
+def pack_weights_kernel(wq, wk, wv, w_keep, w_give):
+    z, _, _, _ = coordinates()
+    zz = z & 1
+    for group in range(2):
+
+        def fill(weights, group=group):
+            weights[:, 0:320] = wq[:, 320 * group : 320 * (group + 1)]
+            weights[:, 320:400] = wk[80 * group : 80 * (group + 1)].T
+            weights[:, 400:480] = wv[80 * group : 80 * (group + 1)].T
+
+        @pl.when(zz == group)
+        def _(fill=fill):
+            fill(w_keep)
+
+        @pl.when(zz != group)
+        def _(fill=fill):
+            fill(w_give)
+
+
+def pack_cache_kernel(tokens, keys, values, kv_own, kv_give, squares):
+    z, _, _, _ = coordinates()
+    zz = z & 1
+    for group in range(2):
+
+        def fill(cache, group=group):
+            cache[0:80] = keys[80 * group : 80 * (group + 1)]
+            cache[80:160] = values[80 * group : 80 * (group + 1)]
+
+        @pl.when(zz == group)
+        def _(fill=fill):
+            fill(kv_own)
+
+        @pl.when(zz != group)
+        def _(fill=fill):
+            fill(kv_give)
+
+    wide_tokens = tokens[...].astype(F32)
+    total = jnp.sum(wide_tokens * wide_tokens, axis=1, keepdims=True)
+    squares[...] = jnp.broadcast_to(total, (128, 128)).T[0:8]
+
+
+def current_kernel(tokens, crossed, squares, squares_z2, out):
+    z, _, y, _ = coordinates()
+    at_home = y == z >> 1
+
+    @pl.when(at_home)
+    def _():
+        out[0:128] = tokens[...]
+
+    @pl.when(jnp.logical_not(at_home))
+    def _():
+        out[0:128] = crossed[...]
+
+    out[128:144] = jnp.zeros((16, 640), BF16)
+    row = lax.broadcasted_iota(jnp.int32, (16, 128), 0)
+    rest = jnp.where(
+        row == 0,
+        jnp.concatenate([squares[...]] * 2, axis=0),
+        jnp.where(row == 1, jnp.concatenate([squares_z2[...]] * 2, axis=0), 0.0),
+    )
+    for part in range(3):
+        rounded = rest.astype(BF16)
+        rest = rest - rounded.astype(F32)
+        out[128:144, 128 * part : 128 * (part + 1)] = rounded
+
+
+def pieces_kernel(weight, swapped, kv_own, here, there, joined):
+    z, x, _, _ = coordinates()
+    same = (z & 1) == x
+
+    @pl.when(same)
+    def _():
+        here[...] = weight[0:160]
+        there[...] = swapped[...]
+
+    @pl.when(jnp.logical_not(same))
+    def _():
+        here[...] = swapped[...]
+        there[...] = weight[0:160]
+
+    joined[:, 0:1024] = kv_own[...]
+    joined[:, 1024:1664] = here[...]
+
+
+def assemble_kernel(near, far, out):
+    _, x, _, _ = coordinates()
+    depth = near.shape[0]
+    out[pl.ds(pl.multiple_of(x * depth, 64), depth), 0:480] = near[...]
+    out[pl.ds(pl.multiple_of((1 - x) * depth, 64), depth), 0:480] = far[...]
+    out[:, 480:] = jnp.zeros((2 * depth, 32), BF16)
+
+
+def stack_kernel(first, second, out):
+    out[0] = first[...]
+    out[1] = second[...]
+
+
+def project_kernel(
+    gain, current, from_z, from_y, from_zy, other, w_rows, w_rows_z,
+    own_out, send_out
+):
+    z, x, y, core = coordinates()
+    half, zz = z >> 1, z & 1
+    at_home = y == half
+    here = zz == core
+    w_here = jnp.where(here, w_rows[...], w_rows_z[...])
+    w_there = jnp.where(here, w_rows_z[...], w_rows[...])
+    both = gain[pl.ds(half, 1)][0]
+    swap = core == 1
+    gain_here = jnp.where(swap, both[1:2], both[0:1])
+    gain_there = jnp.where(swap, both[0:1], both[1:2])
+
+    def stats(block):
+        rows = block[128:144].astype(F32)
+        return rows[:, 0:128] + rows[:, 128:256] + rows[:, 256:384]
+
+    def scaling_of(blocks):
+        total = sum(stats(block) for block in blocks)
+        scale = lax.rsqrt(total / 2560.0 + EPSILON)
+        return jnp.concatenate([scale] * 8, axis=0).T
+
+    scale_z = scaling_of((current, from_y, other.at[0], other.at[2]))
+    scale_z1 = scaling_of((from_z, from_zy, other.at[1], other.at[3]))
+
+    def product(here, there, scale):
+        normed_here = (here[0:128].astype(F32) * scale * gain_here).astype(BF16)
+        normed_there = (there[0:128].astype(F32) * scale * gain_there).astype(BF16)
+        total = jnp.dot(normed_here, w_here, preferred_element_type=F32)
+        total += jnp.dot(normed_there, w_there, preferred_element_type=F32)
+        return total.T[0:480]
+
+    def products(first, second, row, out):
+        for (here, there), scaling, place in (
+            (first, scale_z[:, row : row + 1], zz),
+            (second, scale_z1[:, row : row + 1], 1 - zz),
+        ):
+            result = product(here, there, scaling)
+            lanes = pl.ds(pl.multiple_of(place * 128, 128), 128)
+            out[:, lanes] = result.astype(out.dtype)
+
+    first = ((current, other.at[0]), (from_z, other.at[1]))
+    second = ((from_y, other.at[2]), (from_zy, other.at[3]))
+
+    @pl.when(at_home)
+    def _():
+        products(*second, 1, send_out)
+        products(*first, 0, own_out)
+
+    @pl.when(jnp.logical_not(at_home))
+    def _():
+        products(*first, 1, send_out)
+        products(*second, 0, own_out)
+
+
+def rotary_kernel(own, received, cos, sin, piece_2, q_out, kv_out):
+    total = own[...] + received[...].astype(F32)
+    cos_part = cos[...]
+    sin_part = sin[...]
+    rows = own.shape[1]
+
+    def rotated(first):
+        lower = total[first : first + 40]
+        higher = total[first + 40 : first + 80]
+        return jnp.concatenate(
+            [lower * cos_part - higher * sin_part, higher * cos_part + lower * sin_part], axis=0
+        ).astype(BF16)
+
+    for head in range(4):
+        q_out[:, head * rows : (head + 1) * rows] = rotated(80 * head)
+    kv_out[0:80, 0:256] = rotated(320)
+    kv_out[80:160, 0:256] = total[400:480].astype(BF16)
+    kv_out[:, 256:896] = piece_2[...]
+
+
+def score(keys, queries, allowed, scores, first, top):
+    turned = keys.T
+    count = turned.shape[0]
+    for head in range(4):
+        lanes = slice(head * 256, (head + 1) * 256)
+        part = jnp.dot(turned, queries[:, lanes], preferred_element_type=F32) * EXP2_SCALE
+        if allowed is not None:
+            part = jnp.where(allowed, part, MASKED)
+        scores[first : first + count, lanes] = part
+        top[:, lanes] = jnp.maximum(
+            top[:, lanes], jnp.max(part.reshape(count // 8, 8, 256), axis=0)
+        )
+
+
+def weigh(scores, values_of, block, top, top_old, acc_old, total_old, acc, top_out, total):
+    count = scores.shape[0]
+    for head in range(4):
+        lanes = slice(head * 256, (head + 1) * 256)
+        best = jnp.max(top[:, lanes], axis=0, keepdims=True)
+        if top_old is not None:
+            best = jnp.maximum(best, top_old[0:1, lanes])
+        sums = jnp.zeros((8, 256), F32)
+        mixed = jnp.zeros((80, 256), F32)
+        for first in range(0, count, block):
+            weights = jnp.exp2(scores[first : first + block, lanes] - best)
+            sums += jnp.sum(weights.reshape(block // 8, 8, 256), axis=0)
+            mixed += jnp.dot(
+                values_of(first), weights.astype(BF16), preferred_element_type=F32
+            )
+        sums = jnp.sum(sums, axis=0, keepdims=True)
+        if top_old is not None:
+            rescale = jnp.exp2(top_old[0:1, lanes] - best)
+            sums += total_old[0:1, lanes] * rescale
+            mixed += acc_old[:, lanes] * rescale
+        acc[:, lanes] = mixed
+        top_out[0:1, lanes] = best
+        total[0:1, lanes] = sums
+
+
+def cached_kernel(lengths, offsets, owners, queries, kv_x0, kv_x1, *rest, late):
+    acc, top, total, scores, maxima = rest[-5:]
+    acc_old, top_old, total_old = rest[:3] if late else (None, None, None)
+    z, x, _, _ = coordinates()
+    length, offset, owner = [ref[z >> 1] for ref in (lengths, offsets, owners)]
+    maxima[...] = jnp.full(maxima.shape, FLOOR, F32)
+    lane = lax.broadcasted_iota(jnp.int32, (1, 256), 1)
+    token = (lane // 128 * 2 + x) * 128 + lane % 128
+    oldest = length + token - WIN
+    place = 2 * (z & 1) + x
+    for shard, (flip, source) in enumerate(((2 * late, kv_x0), (2 * late + 1, kv_x1))):
+        begin = (((place ^ flip) - owner) & (GROUP - 1)) * 1024 - offset + length
+        for chunk in range(1024 // CHUNK):
+            first = (begin + chunk * CHUNK) & (WIN - 1)
+            last = first + CHUNK - 1
+            whole = (last < length) & (last < WIN) & (first > length + NEW - 1 - WIN)
+            keys = source[0:80, chunk * CHUNK : (chunk + 1) * CHUNK]
+            row = shard * 1024 + chunk * CHUNK
+
+            @pl.when(whole)
+            def _(keys=keys, row=row):
+                score(keys, queries, None, scores, row, maxima)
+
+            @pl.when(jnp.logical_not(whole))
+            def _(keys=keys, row=row, first=first):
+                slot = lax.broadcasted_iota(jnp.int32, (CHUNK, 128), 0)
+                position = (first + slot) & (WIN - 1)
+                position = jnp.where(position < length, position, -2 * WIN)
+                allowed = jnp.concatenate([position, position], axis=1) > oldest
+                score(keys, queries, allowed, scores, row, maxima)
+
+    def values_of(first):
+        source = (kv_x0, kv_x1)[first // 1024]
+        return source[80:160, first % 1024 : first % 1024 + CHUNK]
+
+    weigh(
+        scores, values_of, CHUNK, maxima, top_old, acc_old, total_old, acc, top, total
+    )
+
+
+def fresh_kernel(
+    queries, kv_mine, kv_other, acc_old, top_old, total_old, out, acc, top, total, scores, maxima
+):
+    _, x, _, _ = coordinates()
+    maxima[...] = jnp.full(maxima.shape, FLOOR, F32)
+    lane = lax.broadcasted_iota(jnp.int32, (1, 256), 1)
+    token = (lane // 128 * 2 + x) * 128 + lane % 128
+    for index, (source, its_x) in enumerate(((kv_mine, x), (kv_other, 1 - x))):
+        row = lax.broadcasted_iota(jnp.int32, (256, 256), 0)
+        key_token = (row // 128 * 2 + its_x) * 128 + row % 128
+        score(source[0:80, 0:256], queries, key_token <= token, scores, index * 256, maxima)
+
+    def values_of(first):
+        return (kv_mine, kv_other)[first // 256][80:160, 0:256]
+
+    weigh(scores, values_of, 256, maxima, top_old, acc_old, total_old, acc, top, total)
+    for head in range(4):
+        lanes = slice(head * 256, (head + 1) * 256)
+        out[head * 80 : (head + 1) * 80] = (acc[:, lanes] / total[0:1, lanes]).astype(BF16)
+
+
+def append_kernel(
+    offsets, owners, kv_mine, kv_other, kv_z, cache_keys, cache_values, put_keys, put_values, fresh
+):
+    z, x, _, _ = coordinates()
+    zz = z & 1
+    offset, owner = offsets[z >> 1], owners[z >> 1]
+    first = ((2 * zz + x - owner) & (GROUP - 1)) * 1024
+    upper = x == 1
+    for head, (mine, other) in enumerate(((kv_mine, kv_other), (kv_z.at[0], kv_z.at[1]))):
+        mine = mine[:, 0:256].astype(F32)
+        other = other[:, 0:256].astype(F32)
+        low = jnp.where(upper, other, mine)
+        high = jnp.where(upper, mine, other)
+        fresh[head, :, 0:128] = low[:, 0:128]
+        fresh[head, :, 128:256] = high[:, 0:128]
+        fresh[head, :, 256:384] = low[:, 128:256]
+        fresh[head, :, 384:512] = high[:, 128:256]
+        fresh[head, :, 512:1024] = jnp.zeros((160, 512), F32)
+    shift = (offset - first) & 1023
+    column = lax.broadcasted_iota(jnp.int32, (80, 1024), 1)
+    written = ((column + first - offset) & (WIN - 1)) < 512
+    for head in range(2):
+        rows = slice(head * 80, (head + 1) * 80)
+        moved = pltpu.roll(fresh[zz ^ head], shift, 1)
+        put_keys[rows] = jnp.where(written, moved[0:80], cache_keys[rows].astype(F32)).astype(BF16)
+        put_values[rows] = jnp.where(
+            written, moved[80:160], cache_values[rows].astype(F32)
+        ).astype(BF16)
+
+
+def output_kernel(
+    own, from_core, from_y, from_yc, mine_0, mine_1, mine_2, mine_3, far_0, far_1, far_2, far_3,
+    out, heads, *, keep
+):
+    z, x, y, core = coordinates()
+    narrow = 2 * y + core
+    tokens = pl.ds(pl.multiple_of(((z & 1) ^ (1 - keep)) * 128, 128), 128)
+    for step, source in enumerate((own, from_core, from_y, from_yc)):
+        heads[step] = source[:, tokens]
+    first = pl.multiple_of(jnp.where((z & 1) == x, 0, 160), 32)
+    second = pl.multiple_of(jnp.where((z & 1) == x, 160, 0), 32)
+    total = jnp.zeros((128, 640), F32)
+    for i, (mine, far) in enumerate(
+        ((mine_0, far_0), (mine_1, far_1), (mine_2, far_2), (mine_3, far_3))
+    ):
+        step = (z ^ i) ^ narrow
+        lanes = slice(1024, 1664) if i == 0 else slice(256, 896) if i == 2 else slice(0, 640)
+        for start, rows in ((first, mine[...]), (second, far[:, lanes])):
+            total += lax.dot_general(
+                heads[step, pl.ds(start, 160)],
+                rows,
+                (((0,), (0,)), ((), ())),
+                preferred_element_type=F32,
+            )
+    out[...] = total.astype(out.dtype)
+
+
+def shards_cube(
+    tokens_in,
+    norm_gain,
+    query_weight,
+    key_weight,
+    value_weight,
+    out_weight,
+    cache_keys,
+    cache_values,
+    cached_len,
+    append_slot,
+    shard_owner,
+):
+    def flip_z(z, x, y, c):
+        return (z ^ 1, x, y, c)
+
+    def flip_x(z, x, y, c):
+        return (z, 1 - x, y, c)
+
+    def flip_y(z, x, y, c):
+        return (z, x, 1 - y, c)
+
+    def flip_core(z, x, y, c):
+        return (z, x, y, 1 - c)
+
+    def flip_half(z, x, y, c):
+        return (z ^ 2, x, y, c)
+
+    crossed = send(tokens_in, lambda z, x, y, c: (z ^ 2, x, 1 - y, c) if y != z // 2 else None)
+    out_swapped = send(out_weight[160:320], flip_x)
+    w_keep, w_give = call(
+        pack_weights_kernel,
+        (shaped((320, 480)), shaped((320, 480))),
+        query_weight,
+        key_weight.T,
+        value_weight.T,
+    )
+    w_z = send(w_give, flip_z)
+    w_keep_x = send(w_keep, flip_x)
+    kv_own, kv_give, squares = call(
+        pack_cache_kernel,
+        (shaped((160, 1024)), shaped((160, 1024)), shaped((8, 128), F32)),
+        tokens_in,
+        cache_keys,
+        cache_values,
+    )
+    half = lax.axis_index("wide") // 4
+    x = lax.axis_index("wide") % 2
+    lane = jnp.arange(256, dtype=jnp.int32)
+    length = jnp.where(half == 0, cached_len[0], cached_len[1])
+    position = length + (lane // 128 * 2 + x) * 128 + lane % 128
+    inverse = ROPE_BASE ** (-(jnp.arange(40, dtype=F32) * (2.0 / HEAD_DIM)))
+    angles = position.astype(F32)[None, :] * inverse[:, None]
+    cos, sin = jnp.cos(angles), jnp.sin(angles)
+    gain = norm_gain.astype(F32).reshape(2, 2, 640)
+
+    squares_z2 = send(squares, flip_half)
+    current = call(
+        current_kernel, shaped((144, 640)), tokens_in, crossed, squares, squares_z2
+    )
+    current, w_z, w_keep_x, kv_own, kv_give = lax.optimization_barrier(
+        (current, w_z, w_keep_x, kv_own, kv_give)
+    )
+    from_z = send(current, flip_z)
+    from_y = send(current, flip_y)
+    from_zy = send(from_z, flip_y)
+    w_z_x = send(w_z, flip_x)
+    piece_0, piece_there, kv_joined = call(
+        pieces_kernel,
+        (shaped((160, 640)), shaped((160, 640)), shaped((160, 1664))),
+        out_weight,
+        out_swapped,
+        kv_own,
+    )
+    blocks = jnp.stack([current, from_z, from_y, from_zy])
+    piece_2 = send(piece_0, flip_half)
+    blocks, cos, sin, gain = lax.optimization_barrier((blocks, cos, sin, gain))
+    other = send(blocks, flip_core)
+    w_rows = call(
+        assemble_kernel,
+        shaped((640, 512)),
+        w_keep,
+        after(w_keep_x, from_z),
+        flops=6000000000,
+    )
+    w_rows_z = call(assemble_kernel, shaped((640, 512)), w_z, w_z_x, flops=11000000000)
+    kv_z = send(after(kv_give, other), flip_z)
+    kv_own_x = send(after(kv_joined, w_rows_z), flip_x)
+
+
+    own_sum, give_sum = call(
+        project_kernel,
+        (shaped((480, 256), F32), shaped((480, 256))),
+        gain,
+        current,
+        from_z,
+        from_y,
+        from_zy,
+        after(other, piece_2),
+        w_rows,
+        w_rows_z,
+    )
+    got_sum = send(give_sum, flip_half)
+    piece_1 = send(after(piece_there, kv_z, give_sum), flip_z)
+    piece_3 = send(after(piece_there, kv_z, give_sum), lambda z, x, y, c: (z ^ 3, x, y, c))
+    got_sum = after(got_sum, kv_z, kv_own_x)
+    kv_z_x = send(after(kv_z, give_sum), flip_x)
+
+    queries, new_kv = call(
+        rotary_kernel,
+        (shaped((80, 1024)), shaped((160, 896))),
+        own_sum,
+        got_sum,
+        cos,
+        sin,
+        piece_2,
+        flops=2_500_000_000,
+    )
+    new_kv_x = send(new_kv, flip_x)
+
+    scalars = (cached_len, append_slot, shard_owner)
+    states = (shaped((80, 1024), F32), shaped((8, 1024), F32), shaped((8, 1024), F32))
+    scratch = [pltpu.VMEM((2048, 1024), F32), pltpu.VMEM((8, 1024), F32)]
+    state = call(
+        functools.partial(cached_kernel, late=0),
+        states,
+        *scalars,
+        queries,
+        kv_own,
+        kv_own_x,
+        scalars=3,
+        scratch=scratch,
+    )
+    state = call(
+        functools.partial(cached_kernel, late=1),
+        states,
+        *scalars,
+        queries,
+        kv_z,
+        kv_z_x,
+        *state,
+        scalars=3,
+        scratch=scratch,
+    )
+    piece_1, piece_3 = after((piece_1, piece_3), state)
+    far_13 = send(call(stack_kernel, shaped((2, 160, 640)), piece_1, piece_3), flip_x)
+    attended = call(
+        fresh_kernel,
+        shaped((320, 256)),
+        queries,
+        new_kv,
+        new_kv_x,
+        *state,
+        scratch=[
+            pltpu.VMEM((80, 1024), F32),
+            pltpu.VMEM((8, 1024), F32),
+            pltpu.VMEM((8, 1024), F32),
+            pltpu.VMEM((512, 1024), F32),
+            pltpu.VMEM((8, 1024), F32),
+        ],
+    )
+
+    new_kv_z = send(after(jnp.stack([new_kv[:, :256], new_kv_x[:, :256]]), attended), flip_z)
+    from_core = send(attended, flip_core)
+    from_y = send(attended, flip_y)
+    from_yc = send(from_y, flip_core)
+    operands = (
+        attended,
+        from_core,
+        from_y,
+        after(from_yc, new_kv_z),
+        piece_0,
+        piece_1,
+        piece_2,
+        piece_3,
+        kv_own_x,
+        far_13[0],
+        new_kv_x,
+        far_13[1],
+    )
+    give, keep = [
+        call(
+            functools.partial(output_kernel, keep=keep),
+            shaped((128, 640), F32 if keep else BF16),
+            *operands,
+            scratch=[pltpu.VMEM((4, 320, 128), BF16)],
+        )
+        for keep in (0, 1)
+    ]
+    got = send(give, flip_z)
+    put_keys, put_values = call(
+        append_kernel,
+        (shaped((160, 1024)), shaped((160, 1024))),
+        append_slot,
+        shard_owner,
+        new_kv,
+        new_kv_x,
+        after(new_kv_z, give),
+        cache_keys,
+        cache_values,
+        scalars=2,
+        scratch=[pltpu.VMEM((2, 160, 1024), F32)],
+    )
+    update = (keep + got.astype(F32)).astype(BF16)
+    return (update, put_keys, put_values)
+
+
 def solution(mesh):
     in_specs = (
         P("wide", "narrow"),
@@ -225,4 +816,6 @@
         P(),
     )
     out_specs = (P("wide", "narrow"), P("narrow", "wide"), P("narrow", "wide"))
+    cube = dict(mesh.shape) == {"wide": 8, "narrow": 4}
+    shards = shards_cube if cube else shards_any
     return jax.shard_map(shards, mesh=mesh, in_specs=in_specs, out_specs=out_specs, check_vma=False)

time: 246 us -> 83.8 us (0.34)
  blocking collectives: 87.4 us -> 0 us
  matrix products: 31.9 us -> 0 us
  other arithmetic: 26.9 us -> 1.06 us
  local copies, waits for them, and re-layouts: 30.8 us -> 5.09 us
  starting transfers between devices: 7.14 us -> 29.3 us
  Pallas kernels: 0 us -> 16.2 us
  between operations: 15.9 us -> 2.15 us
  waiting for transfers between devices: 43.3 us -> 29.7 us
    all_gather x4 -> x0, blocking collectives: 87.4 us -> none  [the longest x1 36.8 us: shards(): lax.all_gather(key_weight, 'wide', axis=0, tiled=True)]
    dot_general x22 -> x0, matrix products: 31.9 us -> none  [the longest x9 12.2 us: step(): jnp.einsum('tgrk,gdk->tgrd', weights.astype(jnp.bfloat16), block_values,...]
    ppermute x8 -> x24, starting transfers between devices: 7.06 us -> 29.3 us  [send(): return lax.ppermute(block, ('wide', 'narrow'), route)]
    pallas_call x0 -> x15, Pallas kernels: none -> 16.2 us  [call(): pl.pallas_call(kernel, out_shape=outs, in_specs=specs, out_specs=jax.tree...]
    dynamic_slice x19 -> x0, local copies, waits for them, and re-layouts: 13.7 us -> none  [the longest x8 6.1 us: step(): block_pos = lax.dynamic_slice_in_dim(key_pos, start, block, 0)]
    ppermute x8 -> x24, waiting for transfers between devices: 42.6 us -> 29.7 us  [send(): return lax.ppermute(block, ('wide', 'narrow'), route)]
    gather x2 -> x0, local copies, waits for them, and re-layouts: 9.89 us -> none  [the longest x1 4.95 us: shards(): jnp.take(key_cols, take_rows, axis=1)]
    select_n x8 -> x0, other arithmetic: 8.59 us -> none  [the longest x6 3.09 us: ordered(): first_half = jnp.where(upper, other, mine)]
  transfers between devices with their start and end apart: 10 -> 24, of which waited for: 4 -> 14; matrix products, arithmetic and copies ran while one was open for 35% -> 1% of each run, Pallas kernels for 0% -> 17%
where the time goes in v1:
time: 83.8 us; the launch traced here: 83.5 us
  waiting for transfers between devices  29.7 us (35%)
  starting transfers between devices  29.3 us (35%)
  Pallas kernels  16.2 us (19%)
  local copies, waits for them, and re-layouts  5.09 us (6%)
  between operations  2.15 us (3%)
  other arithmetic  1.06 us (1%)
    ppermute x24, waiting for transfers between devices, send(): return lax.ppermute(block, ('wide', 'narrow'), route)  29.7 us
    ppermute x24, starting transfers between devices, send(): return lax.ppermute(block, ('wide', 'narrow'), route)  29.3 us
    pallas_call x15, Pallas kernels, call(): pl.pallas_call(kernel, out_shape=outs, in_specs=specs, out_specs=jax.tree...  16.2 us
    unnamed x24, local copies, waits for them, and re-layouts  4.43 us
  transfers between devices with their start and end apart: 24, of which 14 were waited for; matrix products, arithmetic and copies ran while one was open for 1% of the time, Pallas kernels for 17%

profile of v1, /device:TPU:0, one launch (start us, length us, event | category | flops | bytes accessed | tf_op | source)
XLA Modules:
  0.0 83.5 jit_solution(6734843125797913799)
XLA Ops:
  4.7 2.9 %collective-permute-start.3 = (bf16[320,480]{1,0:T(8,128)(2,1)S(1)}, bf16[320,480]{1,0:T(8,128)(2,1)S(1)}, u32[]{:S(2)}, u32[]{:S(2)}) collective-permute-start(bf16[320,480]{1,0:T(8,128)(2,1)S(1)} %get-tuple-element.46.near), channel_id=1, source_target_pairs={{0,4},{1,5},{2,6},{3,7},{4,0},{5,1},{6,2},{7,3},{8,12},{9,13},{10,... | collective-permute-start | bytes 921608 | tf_op jit(solution)/shard_map/ppermute | solution.py:235
  7.6 1.6 %collective-permute-start.2 = (bf16[320,480]{1,0:T(8,128)(2,1)}, bf16[320,480]{1,0:T(8,128)(2,1)S(1)}, u32[]{:S(2)}, u32[]{:S(2)}) collective-permute-start(bf16[320,480]{1,0:T(8,128)(2,1)} %get-tuple-element.45), channel_id=1, source_target_pairs={{0,8},{1,9},{2,10},{3,11},{4,12},{5,13},{6,14},{7,15},{8,0},{9,1},... | collective-permute-start | bytes 921608 | tf_op jit(solution)/shard_map/ppermute | solution.py:235
  11.0 5.2 %collective-permute-start.1 = (f32[8,128]{1,0:T(8,128)S(1)}, f32[8,128]{1,0:T(8,128)S(1)}, u32[]{:S(2)}, u32[]{:S(2)}) collective-permute-start(f32[8,128]{1,0:T(8,128)S(1)} %get-tuple-element.44.squares), channel_id=1, source_target_pairs={{0,16},{1,17},{2,18},{3,19},{4,20},{5,21},{6,22},{7,23},{8,24},{9,... | collective-permute-start | bytes 12296 | tf_op jit(solution)/shard_map/ppermute | solution.py:235
  20.6 2.7 %collective-permute-start.4 = (bf16[144,640]{1,0:T(8,128)(2,1)S(1)}, bf16[144,640]{1,0:T(8,128)(2,1)S(1)}, u32[]{:S(2)}, u32[]{:S(2)}) collective-permute-start(bf16[144,640]{1,0:T(8,128)(2,1)S(1)} %shard_map.131.current), channel_id=1, source_target_pairs={{0,8},{1,9},{2,10},{3,11},{4,12},{5,13},{6,14},{7,15},{8,0},{9,1},... | collective-permute-start | bytes 552968 | tf_op jit(solution)/shard_map/ppermute | solution.py:235
  23.3 1.5 %collective-permute-start.5 = (bf16[144,640]{1,0:T(8,128)(2,1)S(1)}, bf16[144,640]{1,0:T(8,128)(2,1)S(1)}, u32[]{:S(2)}, u32[]{:S(2)}) collective-permute-start(bf16[144,640]{1,0:T(8,128)(2,1)S(1)} %shard_map.131.current), channel_id=1, source_target_pairs={{0,2},{1,3},{2,0},{3,1},{4,6},{5,7},{6,4},{7,5},{8,10},{9,11},{10,... | collective-permute-start | bytes 552968 | tf_op jit(solution)/shard_map/ppermute | solution.py:235
  25.3 1.5 %collective-permute-done.4.from_z = bf16[144,640]{1,0:T(8,128)(2,1)S(1)} collective-permute-done((bf16[144,640]{1,0:T(8,128)(2,1)S(1)}, bf16[144,640]{1,0:T(8,128)(2,1)S(1)}, u32[]{:S(2)}, u32[]{:S(2)}) %collective-permute-start.4) | collective-permute-done | bytes 184352 | tf_op jit(solution)/shard_map/ppermute | solution.py:235
  26.8 1.4 %collective-permute-start.6 = (bf16[144,640]{1,0:T(8,128)(2,1)S(1)}, bf16[144,640]{1,0:T(8,128)(2,1)S(1)}, u32[]{:S(2)}, u32[]{:S(2)}) collective-permute-start(bf16[144,640]{1,0:T(8,128)(2,1)S(1)} %collective-permute-done.4.from_z), channel_id=1, source_target_pairs={{0,2},{1,3},{2,0},{3,1},{4,6},{5,7},{6,4},{7,5},{8,10},{9,11},{10,... | collective-permute-start | bytes 552968 | tf_op jit(solution)/shard_map/ppermute | solution.py:235
  28.6 2.1 %collective-permute-start.9 = (bf16[160,640]{1,0:T(8,128)(2,1)S(1)}, bf16[160,640]{1,0:T(8,128)(2,1)S(1)}, u32[]{:S(2)}, u32[]{:S(2)}) collective-permute-start(bf16[160,640]{1,0:T(8,128)(2,1)S(1)} %get-tuple-element.53.mine_0), channel_id=1, source_target_pairs={{0,16},{1,17},{2,18},{3,19},{4,20},{5,21},{6,22},{7,23},{8,24},{9,... | collective-permute-start | bytes 614408 | tf_op jit(solution)/shard_map/ppermute | solution.py:235
  30.8 2.0 %collective-permute-done.6.from_zy = bf16[144,640]{1,0:T(8,128)(2,1)S(1)} collective-permute-done((bf16[144,640]{1,0:T(8,128)(2,1)S(1)}, bf16[144,640]{1,0:T(8,128)(2,1)S(1)}, u32[]{:S(2)}, u32[]{:S(2)}) %collective-permute-start.6) | collective-permute-done | bytes 184352 | tf_op jit(solution)/shard_map/ppermute | solution.py:235
  33.7 1.5 %collective-permute-done.7.other = bf16[4,144,640]{2,1,0:T(8,128)(2,1)S(1)} collective-permute-done((bf16[4,144,640]{2,1,0:T(8,128)(2,1)S(1)}, bf16[4,144,640]{2,1,0:T(8,128)(2,1)S(1)}, u32[]{:S(2)}, u32[]{:S(2)}) %collective-permute-start.7) | collective-permute-done | bytes 737312 | tf_op jit(solution)/shard_map/ppermute | solution.py:235
  35.2 1.6 %collective-permute-start.12 = (bf16[160,1024]{1,0:T(8,128)(2,1)S(1)}, bf16[160,1024]{1,0:T(8,128)(2,1)S(1)}, u32[]{:S(2)}, u32[]{:S(2)}) collective-permute-start(bf16[160,1024]{1,0:T(8,128)(2,1)S(1)} %get-tuple-element.61), channel_id=1, source_target_pairs={{0,8},{1,9},{2,10},{3,11},{4,12},{5,13},{6,14},{7,15},{8,0},{9,1},... | collective-permute-start | bytes 983048 | tf_op jit(solution)/shard_map/ppermute | solution.py:235
  36.9 1.5 %collective-permute-done.9.piece_2.mine_2 = bf16[160,640]{1,0:T(8,128)(2,1)S(1)} collective-permute-done((bf16[160,640]{1,0:T(8,128)(2,1)S(1)}, bf16[160,640]{1,0:T(8,128)(2,1)S(1)}, u32[]{:S(2)}, u32[]{:S(2)}) %collective-permute-start.9) | collective-permute-done | bytes 204832 | tf_op jit(solution)/shard_map/ppermute | solution.py:235
  38.4 1.4 %shard_map.136 = (f32[480,256]{1,0:T(8,128)S(1)}, bf16[480,256]{1,0:T(8,128)(2,1)S(1)}) custom-call(f32[2,2,640]{2,1,0:T(2,128)S(1)} %reshape.47.gain, bf16[144,640]{1,0:T(8,128)(2,1)S(1)} %shard_map.131.current, bf16[144,640]{1,0:T(8,128)(2,1)S(1)} %collective-permute-done.4.from_z, bf16[144,640]{1,0:T(8,128)(2,1)S(1)} %collective-permute-done.5.from_y, ...), custom_call_target="tpu_custom_call" | custom-call | flops 1 | bytes 1 | tf_op jit(solution)/shard_map/pallas_call | solution.py:245
  39.9 7.8 %collective-permute-done.13.kv_x1.far_0 = bf16[160,1664]{1,0:T(8,128)(2,1)S(1)} collective-permute-done((bf16[160,1664]{1,0:T(8,128)(2,1)S(1)}, bf16[160,1664]{1,0:T(8,128)(2,1)S(1)}, u32[]{:S(2)}, u32[]{:S(2)}) %collective-permute-start.13) | collective-permute-done | bytes 532512 | tf_op jit(solution)/shard_map/ppermute | solution.py:235
  47.7 4.9 %collective-permute-done.11.received = bf16[480,256]{1,0:T(8,128)(2,1)S(1)} collective-permute-done((bf16[480,256]{1,0:T(8,128)(2,1)S(1)}, bf16[480,256]{1,0:T(8,128)(2,1)S(1)}, u32[]{:S(2)}, u32[]{:S(2)}) %collective-permute-start.11) | collective-permute-done | bytes 245792 | tf_op jit(solution)/shard_map/ppermute | solution.py:235
  53.2 1.6 %collective-permute-start.14 = (bf16[160,896]{1,0:T(8,128)(2,1)S(1)}, bf16[160,896]{1,0:T(8,128)(2,1)S(1)}, u32[]{:S(2)}, u32[]{:S(2)}) collective-permute-start(bf16[160,896]{1,0:T(8,128)(2,1)S(1)} %get-tuple-element.68.kv_mine), channel_id=1, source_target_pairs={{0,4},{1,5},{2,6},{3,7},{4,0},{5,1},{6,2},{7,3},{8,12},{9,13},{10,... | collective-permute-start | bytes 860168 | tf_op jit(solution)/shard_map/ppermute | solution.py:235
  54.9 2.0 %collective-permute-start.21 = (bf16[160,640]{1,0:T(8,128)(2,1)S(1)}, bf16[160,640]{1,0:T(8,128)(2,1)S(1)}, u32[]{:S(2)}, u32[]{:S(2)}) collective-permute-start(bf16[160,640]{1,0:T(8,128)(2,1)S(1)} %get-tuple-element.79), channel_id=1, source_target_pairs={{0,24},{1,25},{2,26},{3,27},{4,28},{5,29},{6,30},{7,31},{8,16},{9,... | collective-permute-start | bytes 614408 | tf_op jit(solution)/shard_map/ppermute | solution.py:235
  56.9 4.2 %shard_map.138 = (f32[80,1024]{1,0:T(8,128)S(1)}, f32[8,1024]{1,0:T(8,128)S(1)}, f32[8,1024]{1,0:T(8,128)S(1)}) custom-call(s32[2]{0:T(128)S(1)} %copy-done.8, s32[2]{0:T(128)S(1)} %copy-done.9, s32[2]{0:T(128)S(1)} %copy-done.10, bf16[80,1024]{1,0:T(8,128)(2,1)S(1)} %get-tuple-element.67.queries, bf16[160,1024]{1,0:T(8,128)(2,1)S(1)} %get-tuple-element.52.kv_own.kv_x0, ...), custom_call_target="tpu_custom_call" | custom-call | flops 1 | bytes 1 | tf_op jit(solution)/shard_map/pallas_call | solution.py:245
  61.1 1.5 %collective-permute-done.15.kv_x1 = bf16[160,1024]{1,0:T(8,128)(2,1)S(1)} collective-permute-done((bf16[160,1024]{1,0:T(8,128)(2,1)S(1)}, bf16[160,1024]{1,0:T(8,128)(2,1)S(1)}, u32[]{:S(2)}, u32[]{:S(2)}) %collective-permute-start.15) | collective-permute-done | bytes 327712 | tf_op jit(solution)/shard_map/ppermute | solution.py:235
  62.6 4.4 %shard_map.139 = (f32[80,1024]{1,0:T(8,128)S(1)}, f32[8,1024]{1,0:T(8,128)S(1)}, f32[8,1024]{1,0:T(8,128)S(1)}) custom-call(s32[2]{0:T(128)S(1)} %copy-done.8, s32[2]{0:T(128)S(1)} %copy-done.9, s32[2]{0:T(128)S(1)} %copy-done.10, bf16[80,1024]{1,0:T(8,128)(2,1)S(1)} %get-tuple-element.67.queries, bf16[160,1024]{1,0:T(8,128)(2,1)S(1)} %collective-permute-done.12.kv_x0, ...), custom_call_target="tpu_custom_call" | custom-call | flops 1 | bytes 1 | tf_op jit(solution)/shard_map/pallas_call | solution.py:245
  69.0 1.3 %collective-permute-start.19 = (bf16[2,160,256]{2,1,0:T(8,128)(2,1)S(1)}, bf16[2,160,256]{2,1,0:T(8,128)(2,1)S(1)}, u32[]{:S(2)}, u32[]{:S(2)}) collective-permute-start(bf16[2,160,256]{2,1,0:T(8,128)(2,1)S(1)} %pad_maximum_fusion.1), channel_id=1, source_target_pairs={{0,8},{1,9},{2,10},{3,11},{4,12},{5,13},{6,14},{7,15},{8,0},{9,1},... | collective-permute-start | bytes 491528 | tf_op jit(solution)/shard_map/ppermute | solution.py:235
  70.3 3.8 %collective-permute-done.17.from_y = bf16[320,256]{1,0:T(8,128)(2,1)S(1)} collective-permute-done((bf16[320,256]{1,0:T(8,128)(2,1)S(1)}, bf16[320,256]{1,0:T(8,128)(2,1)S(1)}, u32[]{:S(2)}, u32[]{:S(2)}) %collective-permute-start.17) | collective-permute-done | bytes 163872 | tf_op jit(solution)/shard_map/ppermute | solution.py:235
  78.0 2.0 %shard_map.144 = (bf16[160,1024]{1,0:T(8,128)(2,1)}, bf16[160,1024]{1,0:T(8,128)(2,1)}) custom-call(s32[2]{0:T(128)S(1)} %copy-done.9, s32[2]{0:T(128)S(1)} %copy-done.10, bf16[160,896]{1,0:T(8,128)(2,1)S(1)} %get-tuple-element.68.kv_mine, bf16[160,896]{1,0:T(8,128)(2,1)S(1)} %collective-permute-done.14.kv_other.far_2, ...), custom_call_target="tpu_custom_call" | custom-call | flops 1 | bytes 1 | tf_op jit(solution)/shard_map/pallas_call | solution.py:245
  80.0 2.8 %collective-permute-done.23 = bf16[128,640]{1,0:T(8,128)(2,1)S(1)} collective-permute-done((bf16[128,640]{1,0:T(8,128)(2,1)S(1)}, bf16[128,640]{1,0:T(8,128)(2,1)S(1)}, u32[]{:S(2)}, u32[]{:S(2)}) %collective-permute-start.23) | collective-permute-done | bytes 163872 | tf_op jit(solution)/shard_map/ppermute | solution.py:235
  (75 shorter events, 18.4 us)
Async XLA Ops:
  4.7 15.1 %collective-permute-start.3 = (bf16[320,480]{1,0:T(8,128)(2,1)S(1)}, bf16[320,480]{1,0:T(8,128)(2,1)S(1)}, u32[]{:S(2)}, u32[]{:S(2)}) collective-permute-start(bf16[320,480]{1,0:T(8,128)(2,1)S(1)} %get-tuple-element.46.near), channel_id=1, source_target_pairs={{0,4},{1,5},{2,6},{3,7},{4,0},{5,1},{6,2},{7,3},{8,12},{9,13},{10,... | collective-permute-start | bytes 921608 | tf_op jit(solution)/shard_map/ppermute | solution.py:235
  7.6 13.0 %collective-permute-start.2 = (bf16[320,480]{1,0:T(8,128)(2,1)}, bf16[320,480]{1,0:T(8,128)(2,1)S(1)}, u32[]{:S(2)}, u32[]{:S(2)}) collective-permute-start(bf16[320,480]{1,0:T(8,128)(2,1)} %get-tuple-element.45), channel_id=1, source_target_pairs={{0,8},{1,9},{2,10},{3,11},{4,12},{5,13},{6,14},{7,15},{8,0},{9,1},... | collective-permute-start | bytes 921608 | tf_op jit(solution)/shard_map/ppermute | solution.py:235
  9.2 10.6 %collective-permute-start = (bf16[128,640]{1,0:T(8,128)(2,1)}, bf16[128,640]{1,0:T(8,128)(2,1)S(1)}, u32[]{:S(2)}, u32[]{:S(2)}) collective-permute-start(bf16[128,640]{1,0:T(8,128)(2,1)} %tokens.3), channel_id=1, source_target_pairs={{2,16},{3,17},{6,20},{7,21},{10,24},{11,25},{14,28},{15,29},{16,2}... | collective-permute-start | bytes 491528 | tf_op jit(solution)/shard_map/ppermute | solution.py:235
  11.0 8.8 %collective-permute-start.1 = (f32[8,128]{1,0:T(8,128)S(1)}, f32[8,128]{1,0:T(8,128)S(1)}, u32[]{:S(2)}, u32[]{:S(2)}) collective-permute-start(f32[8,128]{1,0:T(8,128)S(1)} %get-tuple-element.44.squares), channel_id=1, source_target_pairs={{0,16},{1,17},{2,18},{3,19},{4,20},{5,21},{6,22},{7,23},{8,24},{9,... | collective-permute-start | bytes 12296 | tf_op jit(solution)/shard_map/ppermute | solution.py:235
  16.2 12.2 %collective-permute-start.8 = (bf16[160,640]{1,0:T(8,128)(2,1)S(1)}, bf16[160,640]{1,0:T(8,128)(2,1)S(1)}, u32[]{:S(2)}, u32[]{:S(2)}) collective-permute-start(bf16[160,640]{1,0:T(8,128)(2,1)S(1)} %slice.23), channel_id=1, source_target_pairs={{0,4},{1,5},{2,6},{3,7},{4,0},{5,1},{6,2},{7,3},{8,12},{9,13},{10,... | collective-permute-start | bytes 614408 | tf_op jit(solution)/shard_map/ppermute | solution.py:235
  20.6 6.2 %collective-permute-start.4 = (bf16[144,640]{1,0:T(8,128)(2,1)S(1)}, bf16[144,640]{1,0:T(8,128)(2,1)S(1)}, u32[]{:S(2)}, u32[]{:S(2)}) collective-permute-start(bf16[144,640]{1,0:T(8,128)(2,1)S(1)} %shard_map.131.current), channel_id=1, source_target_pairs={{0,8},{1,9},{2,10},{3,11},{4,12},{5,13},{6,14},{7,15},{8,0},{9,1},... | collective-permute-start | bytes 552968 | tf_op jit(solution)/shard_map/ppermute | solution.py:235
  23.3 7.5 %collective-permute-start.5 = (bf16[144,640]{1,0:T(8,128)(2,1)S(1)}, bf16[144,640]{1,0:T(8,128)(2,1)S(1)}, u32[]{:S(2)}, u32[]{:S(2)}) collective-permute-start(bf16[144,640]{1,0:T(8,128)(2,1)S(1)} %shard_map.131.current), channel_id=1, source_target_pairs={{0,2},{1,3},{2,0},{3,1},{4,6},{5,7},{6,4},{7,5},{8,10},{9,11},{10,... | collective-permute-start | bytes 552968 | tf_op jit(solution)/shard_map/ppermute | solution.py:235
  24.8 8.2 %collective-permute-start.10 = (bf16[320,480]{1,0:T(8,128)(2,1)S(1)}, bf16[320,480]{1,0:T(8,128)(2,1)S(1)}, u32[]{:S(2)}, u32[]{:S(2)}) collective-permute-start(bf16[320,480]{1,0:T(8,128)(2,1)S(1)} %collective-permute-done.2.near), channel_id=1, source_target_pairs={{0,4},{1,5},{2,6},{3,7},{4,0},{5,1},{6,2},{7,3},{8,12},{9,13},{10,... | collective-permute-start | bytes 921608 | tf_op jit(solution)/shard_map/ppermute | solution.py:235
  26.8 6.0 %collective-permute-start.6 = (bf16[144,640]{1,0:T(8,128)(2,1)S(1)}, bf16[144,640]{1,0:T(8,128)(2,1)S(1)}, u32[]{:S(2)}, u32[]{:S(2)}) collective-permute-start(bf16[144,640]{1,0:T(8,128)(2,1)S(1)} %collective-permute-done.4.from_z), channel_id=1, source_target_pairs={{0,2},{1,3},{2,0},{3,1},{4,6},{5,7},{6,4},{7,5},{8,10},{9,11},{10,... | collective-permute-start | bytes 552968 | tf_op jit(solution)/shard_map/ppermute | solution.py:235
  28.6 9.8 %collective-permute-start.9 = (bf16[160,640]{1,0:T(8,128)(2,1)S(1)}, bf16[160,640]{1,0:T(8,128)(2,1)S(1)}, u32[]{:S(2)}, u32[]{:S(2)}) collective-permute-start(bf16[160,640]{1,0:T(8,128)(2,1)S(1)} %get-tuple-element.53.mine_0), channel_id=1, source_target_pairs={{0,16},{1,17},{2,18},{3,19},{4,20},{5,21},{6,22},{7,23},{8,24},{9,... | collective-permute-start | bytes 614408 | tf_op jit(solution)/shard_map/ppermute | solution.py:235
  32.9 2.3 %collective-permute-start.7 = (bf16[4,144,640]{2,1,0:T(8,128)(2,1)S(1)}, bf16[4,144,640]{2,1,0:T(8,128)(2,1)S(1)}, u32[]{:S(2)}, u32[]{:S(2)}) collective-permute-start(bf16[4,144,640]{2,1,0:T(8,128)(2,1)S(1)} %pad_maximum_fusion), channel_id=1, source_target_pairs={{0,1},{1,0},{2,3},{3,2},{4,5},{5,4},{6,7},{7,6},{8,9},{9,8},{10,11... | collective-permute-start | bytes 2211848 | tf_op jit(solution)/shard_map/ppermute | solution.py:235
  33.1 14.6 %collective-permute-start.13 = (bf16[160,1664]{1,0:T(8,128)(2,1)S(1)}, bf16[160,1664]{1,0:T(8,128)(2,1)S(1)}, u32[]{:S(2)}, u32[]{:S(2)}) collective-permute-start(bf16[160,1664]{1,0:T(8,128)(2,1)S(1)} %get-tuple-element.63), channel_id=1, source_target_pairs={{0,4},{1,5},{2,6},{3,7},{4,0},{5,1},{6,2},{7,3},{8,12},{9,13},{10,... | collective-permute-start | bytes 1597448 | tf_op jit(solution)/shard_map/ppermute | solution.py:235
  35.2 17.4 %collective-permute-start.12 = (bf16[160,1024]{1,0:T(8,128)(2,1)S(1)}, bf16[160,1024]{1,0:T(8,128)(2,1)S(1)}, u32[]{:S(2)}, u32[]{:S(2)}) collective-permute-start(bf16[160,1024]{1,0:T(8,128)(2,1)S(1)} %get-tuple-element.61), channel_id=1, source_target_pairs={{0,8},{1,9},{2,10},{3,11},{4,12},{5,13},{6,14},{7,15},{8,0},{9,1},... | collective-permute-start | bytes 983048 | tf_op jit(solution)/shard_map/ppermute | solution.py:235
  39.8 12.8 %collective-permute-start.11 = (bf16[480,256]{1,0:T(8,128)(2,1)S(1)}, bf16[480,256]{1,0:T(8,128)(2,1)S(1)}, u32[]{:S(2)}, u32[]{:S(2)}) collective-permute-start(bf16[480,256]{1,0:T(8,128)(2,1)S(1)} %get-tuple-element.59), channel_id=1, source_target_pairs={{0,16},{1,17},{2,18},{3,19},{4,20},{5,21},{6,22},{7,23},{8,24},{9,... | collective-permute-start | bytes 737288 | tf_op jit(solution)/shard_map/ppermute | solution.py:235
  52.6 10.0 %collective-permute-start.15 = (bf16[160,1024]{1,0:T(8,128)(2,1)S(1)}, bf16[160,1024]{1,0:T(8,128)(2,1)S(1)}, u32[]{:S(2)}, u32[]{:S(2)}) collective-permute-start(bf16[160,1024]{1,0:T(8,128)(2,1)S(1)} %collective-permute-done.12.kv_x0), channel_id=1, source_target_pairs={{0,4},{1,5},{2,6},{3,7},{4,0},{5,1},{6,2},{7,3},{8,12},{9,13},{10,... | collective-permute-start | bytes 983048 | tf_op jit(solution)/shard_map/ppermute | solution.py:235
  53.2 14.4 %collective-permute-start.14 = (bf16[160,896]{1,0:T(8,128)(2,1)S(1)}, bf16[160,896]{1,0:T(8,128)(2,1)S(1)}, u32[]{:S(2)}, u32[]{:S(2)}) collective-permute-start(bf16[160,896]{1,0:T(8,128)(2,1)S(1)} %get-tuple-element.68.kv_mine), channel_id=1, source_target_pairs={{0,4},{1,5},{2,6},{3,7},{4,0},{5,1},{6,2},{7,3},{8,12},{9,13},{10,... | collective-permute-start | bytes 860168 | tf_op jit(solution)/shard_map/ppermute | solution.py:235
  54.8 12.1 %collective-permute-start.20 = (bf16[160,640]{1,0:T(8,128)(2,1)S(1)}, bf16[160,640]{1,0:T(8,128)(2,1)S(1)}, u32[]{:S(2)}, u32[]{:S(2)}) collective-permute-start(bf16[160,640]{1,0:T(8,128)(2,1)S(1)} %get-tuple-element.79), channel_id=1, source_target_pairs={{0,8},{1,9},{2,10},{3,11},{4,12},{5,13},{6,14},{7,15},{8,0},{9,1},... | collective-permute-start | bytes 614408 | tf_op jit(solution)/shard_map/ppermute | solution.py:235
  54.9 12.0 %collective-permute-start.21 = (bf16[160,640]{1,0:T(8,128)(2,1)S(1)}, bf16[160,640]{1,0:T(8,128)(2,1)S(1)}, u32[]{:S(2)}, u32[]{:S(2)}) collective-permute-start(bf16[160,640]{1,0:T(8,128)(2,1)S(1)} %get-tuple-element.79), channel_id=1, source_target_pairs={{0,24},{1,25},{2,26},{3,27},{4,28},{5,29},{6,30},{7,31},{8,16},{9,... | collective-permute-start | bytes 614408 | tf_op jit(solution)/shard_map/ppermute | solution.py:235
  67.0 8.5 %collective-permute-start.22 = (bf16[2,160,640]{2,1,0:T(8,128)(2,1)S(1)}, bf16[2,160,640]{2,1,0:T(8,128)(2,1)S(1)}, u32[]{:S(2)}, u32[]{:S(2)}) collective-permute-start(bf16[2,160,640]{2,1,0:T(8,128)(2,1)S(1)} %shard_map.141), channel_id=1, source_target_pairs={{0,4},{1,5},{2,6},{3,7},{4,0},{5,1},{6,2},{7,3},{8,12},{9,13},{10,... | collective-permute-start | bytes 1228808 | tf_op jit(solution)/shard_map/ppermute | solution.py:235
  68.7 5.4 %collective-permute-start.17 = (bf16[320,256]{1,0:T(8,128)(2,1)S(1)}, bf16[320,256]{1,0:T(8,128)(2,1)S(1)}, u32[]{:S(2)}, u32[]{:S(2)}) collective-permute-start(bf16[320,256]{1,0:T(8,128)(2,1)S(1)} %shard_map.140.own), channel_id=1, source_target_pairs={{0,2},{1,3},{2,0},{3,1},{4,6},{5,7},{6,4},{7,5},{8,10},{9,11},{10,... | collective-permute-start | bytes 491528 | tf_op jit(solution)/shard_map/ppermute | solution.py:235
  69.0 5.5 %collective-permute-start.19 = (bf16[2,160,256]{2,1,0:T(8,128)(2,1)S(1)}, bf16[2,160,256]{2,1,0:T(8,128)(2,1)S(1)}, u32[]{:S(2)}, u32[]{:S(2)}) collective-permute-start(bf16[2,160,256]{2,1,0:T(8,128)(2,1)S(1)} %pad_maximum_fusion.1), channel_id=1, source_target_pairs={{0,8},{1,9},{2,10},{3,11},{4,12},{5,13},{6,14},{7,15},{8,0},{9,1},... | collective-permute-start | bytes 491528 | tf_op jit(solution)/shard_map/ppermute | solution.py:235
  74.1 1.4 %collective-permute-start.18 = (bf16[320,256]{1,0:T(8,128)(2,1)S(1)}, bf16[320,256]{1,0:T(8,128)(2,1)S(1)}, u32[]{:S(2)}, u32[]{:S(2)}) collective-permute-start(bf16[320,256]{1,0:T(8,128)(2,1)S(1)} %collective-permute-done.17.from_y), channel_id=1, source_target_pairs={{0,1},{1,0},{2,3},{3,2},{4,5},{5,4},{6,7},{7,6},{8,9},{9,8},{10,11... | collective-permute-start | bytes 491528 | tf_op jit(solution)/shard_map/ppermute | solution.py:235
  74.1 1.6 %collective-permute-start.16 = (bf16[320,256]{1,0:T(8,128)(2,1)S(1)}, bf16[320,256]{1,0:T(8,128)(2,1)S(1)}, u32[]{:S(2)}, u32[]{:S(2)}) collective-permute-start(bf16[320,256]{1,0:T(8,128)(2,1)S(1)} %shard_map.140.own), channel_id=1, source_target_pairs={{0,1},{1,0},{2,3},{3,2},{4,5},{5,4},{6,7},{7,6},{8,9},{9,8},{10,11... | collective-permute-start | bytes 491528 | tf_op jit(solution)/shard_map/ppermute | solution.py:235
  76.4 6.4 %collective-permute-start.23 = (bf16[128,640]{1,0:T(8,128)(2,1)S(1)}, bf16[128,640]{1,0:T(8,128)(2,1)S(1)}, u32[]{:S(2)}, u32[]{:S(2)}) collective-permute-start(bf16[128,640]{1,0:T(8,128)(2,1)S(1)} %shard_map.143), channel_id=1, source_target_pairs={{0,8},{1,9},{2,10},{3,11},{4,12},{5,13},{6,14},{7,15},{8,0},{9,1},... | collective-permute-start | bytes 491528 | tf_op jit(solution)/shard_map/ppermute | solution.py:235
  (12 other events, 44.7 us)

commit v2 on v1

--- a/solution.py
+++ b/solution.py
@@ -239,16 +239,16 @@
     return lax.optimization_barrier((block, *earlier))[0]
 
 
-def call(kernel, outs, *args, scalars=0, scratch=(), flops=1):
+def call(kernel, outs, *args, scalars=0, scratch=(), flops=1, space=pltpu.VMEM, room=40):
     specs = [pl.BlockSpec(memory_space=pltpu.SMEM)] * scalars
-    specs += [pl.BlockSpec(memory_space=pltpu.VMEM)] * (len(args) - scalars)
+    specs += [pl.BlockSpec(memory_space=space)] * (len(args) - scalars)
     return pl.pallas_call(
         kernel,
         out_shape=outs,
         in_specs=specs,
         out_specs=jax.tree.map(lambda _: pl.BlockSpec(memory_space=pltpu.VMEM), outs),
         scratch_shapes=scratch,
-        compiler_params=pltpu.CompilerParams(vmem_limit_bytes=40 * 1024 * 1024),
+        compiler_params=pltpu.CompilerParams(vmem_limit_bytes=room * 1024 * 1024),
         cost_estimate=pl.CostEstimate(flops=flops, bytes_accessed=1, transcendentals=0),
     )(*args)
 
@@ -263,7 +263,15 @@
     return wide >> 1, wide & 1, narrow >> 1, narrow & 1
 
 
-def pack_weights_kernel(wq, wk, wv, w_keep, w_give):
+def pack_weights_kernel(wq_far, wk_far, wv_far, w_keep, w_give, wq, wk, wv, arrived):
+    copies = [
+        pltpu.make_async_copy(source, target, arrived.at[index])
+        for index, (source, target) in enumerate(((wq_far, wq), (wk_far, wk), (wv_far, wv)))
+    ]
+    for copy in copies:
+        copy.start()
+    for copy in copies:
+        copy.wait()
     z, _, _, _ = coordinates()
     zz = z & 1
     for group in range(2):
@@ -630,6 +638,14 @@
         query_weight,
         key_weight.T,
         value_weight.T,
+        space=pltpu.HBM,
+        room=62,
+        scratch=[
+            pltpu.VMEM((320, 640), BF16),
+            pltpu.VMEM((160, 320), BF16),
+            pltpu.VMEM((160, 320), BF16),
+            pltpu.SemaphoreType.DMA((3,)),
+        ],
     )
     w_z = send(w_give, flip_z)
     w_keep_x = send(w_keep, flip_x)
@@ -680,7 +696,7 @@
         flops=6000000000,
     )
     w_rows_z = call(assemble_kernel, shaped((640, 512)), w_z, w_z_x, flops=11000000000)
-    kv_z = send(after(kv_give, other), flip_z)
+    kv_z = send(after(kv_give, from_z), flip_z)
     kv_own_x = send(after(kv_joined, w_rows_z), flip_x)
 
 
@@ -697,8 +713,6 @@
         w_rows_z,
     )
     got_sum = send(give_sum, flip_half)
-    piece_1 = send(after(piece_there, kv_z, give_sum), flip_z)
-    piece_3 = send(after(piece_there, kv_z, give_sum), lambda z, x, y, c: (z ^ 3, x, y, c))
     got_sum = after(got_sum, kv_z, kv_own_x)
     kv_z_x = send(after(kv_z, give_sum), flip_x)
 
@@ -713,6 +727,8 @@
         flops=2_500_000_000,
     )
     new_kv_x = send(new_kv, flip_x)
+    piece_1 = send(after(piece_there, queries), flip_z)
+    piece_3 = send(after(piece_there, queries), lambda z, x, y, c: (z ^ 3, x, y, c))
 
     scalars = (cached_len, append_slot, shard_owner)
     states = (shaped((80, 1024), F32), shaped((8, 1024), F32), shaped((8, 1024), F32))

time: 83.8 us -> 79.3 us (0.946)
  waiting for transfers between devices: 29.7 us -> 23.7 us
  starting transfers between devices: 29.3 us -> 31.8 us
  local copies, waits for them, and re-layouts: 5.09 us -> 3.17 us
  Pallas kernels: 16.2 us -> 17.1 us
    ppermute x24, waiting for transfers between devices: 29.7 us -> 23.7 us  [send(): return lax.ppermute(block, ('wide', 'narrow'), route)]
    unnamed x24 -> x18, local copies, waits for them, and re-layouts: 4.43 us -> 1.82 us
    ppermute x24, starting transfers between devices: 29.3 us -> 31.8 us  [send(): return lax.ppermute(block, ('wide', 'narrow'), route)]
    pallas_call x15, Pallas kernels: 16.2 us -> 17.1 us  [call(): pl.pallas_call(kernel, out_shape=outs, in_specs=specs, out_specs=jax.tree...]
  transfers between devices with their start and end apart: 24 -> 24, of which waited for: 14 -> 12; matrix products, arithmetic and copies ran while one was open for 1% -> 2% of each run, Pallas kernels for 17% -> 18%
where the time goes in v2:
time: 79.3 us; the launch traced here: 79.1 us
  starting transfers between devices  31.8 us (40%)
  waiting for transfers between devices  23.7 us (30%)
  Pallas kernels  17.1 us (22%)
  local copies, waits for them, and re-layouts  3.17 us (4%)
  between operations  2.22 us (3%)
  other arithmetic  1.07 us (1%)
    ppermute x24, starting transfers between devices, send(): return lax.ppermute(block, ('wide', 'narrow'), route)  31.8 us
    ppermute x24, waiting for transfers between devices, send(): return lax.ppermute(block, ('wide', 'narrow'), route)  23.7 us
    pallas_call x15, Pallas kernels, call(): pl.pallas_call(kernel, out_shape=outs, in_specs=specs, out_specs=jax.tree...  17.1 us
    unnamed x18, local copies, waits for them, and re-layouts  1.82 us
  transfers between devices with their start and end apart: 24, of which 12 were waited for; matrix products, arithmetic and copies ran while one was open for 2% of the time, Pallas kernels for 18%

profile of v2, /device:TPU:0, one launch (start us, length us, event | category | flops | bytes accessed | tf_op | source)
XLA Modules:
  0.0 79.1 jit_solution(13440829383016980554)
XLA Ops:
  0.7 2.5 %shard_map.132 = (bf16[320,480]{1,0:T(8,128)(2,1)}, bf16[320,480]{1,0:T(8,128)(2,1)}) custom-call(bf16[320,640]{1,0:T(8,128)(2,1)} %wq_far.1, bf16[160,320]{1,0:T(8,128)(2,1)} %bitcast.20, bf16[160,320]{1,0:T(8,128)(2,1)} %bitcast.21), custom_call_target="tpu_custom_call" | custom-call | flops 1 | bytes 1 | tf_op jit(solution)/shard_map/pallas_call | solution.py:245
  3.2 3.0 %collective-permute-start.3 = (bf16[320,480]{1,0:T(8,128)(2,1)}, bf16[320,480]{1,0:T(8,128)(2,1)S(1)}, u32[]{:S(2)}, u32[]{:S(2)}) collective-permute-start(bf16[320,480]{1,0:T(8,128)(2,1)} %get-tuple-element.46.near), channel_id=1, source_target_pairs={{0,4},{1,5},{2,6},{3,7},{4,0},{5,1},{6,2},{7,3},{8,12},{9,13},{10,... | collective-permute-start | bytes 921608 | tf_op jit(solution)/shard_map/ppermute | solution.py:235
  6.2 1.6 %collective-permute-start.2 = (bf16[320,480]{1,0:T(8,128)(2,1)}, bf16[320,480]{1,0:T(8,128)(2,1)S(1)}, u32[]{:S(2)}, u32[]{:S(2)}) collective-permute-start(bf16[320,480]{1,0:T(8,128)(2,1)} %get-tuple-element.45), channel_id=1, source_target_pairs={{0,8},{1,9},{2,10},{3,11},{4,12},{5,13},{6,14},{7,15},{8,0},{9,1},... | collective-permute-start | bytes 921608 | tf_op jit(solution)/shard_map/ppermute | solution.py:235
  9.5 5.2 %collective-permute-start.1 = (f32[8,128]{1,0:T(8,128)S(1)}, f32[8,128]{1,0:T(8,128)S(1)}, u32[]{:S(2)}, u32[]{:S(2)}) collective-permute-start(f32[8,128]{1,0:T(8,128)S(1)} %get-tuple-element.44.squares), channel_id=1, source_target_pairs={{0,16},{1,17},{2,18},{3,19},{4,20},{5,21},{6,22},{7,23},{8,24},{9,... | collective-permute-start | bytes 12296 | tf_op jit(solution)/shard_map/ppermute | solution.py:235
  19.2 2.7 %collective-permute-start.4 = (bf16[144,640]{1,0:T(8,128)(2,1)S(1)}, bf16[144,640]{1,0:T(8,128)(2,1)S(1)}, u32[]{:S(2)}, u32[]{:S(2)}) collective-permute-start(bf16[144,640]{1,0:T(8,128)(2,1)S(1)} %shard_map.131.current), channel_id=1, source_target_pairs={{0,8},{1,9},{2,10},{3,11},{4,12},{5,13},{6,14},{7,15},{8,0},{9,1},... | collective-permute-start | bytes 552968 | tf_op jit(solution)/shard_map/ppermute | solution.py:235
  21.9 1.5 %collective-permute-start.5 = (bf16[144,640]{1,0:T(8,128)(2,1)S(1)}, bf16[144,640]{1,0:T(8,128)(2,1)S(1)}, u32[]{:S(2)}, u32[]{:S(2)}) collective-permute-start(bf16[144,640]{1,0:T(8,128)(2,1)S(1)} %shard_map.131.current), channel_id=1, source_target_pairs={{0,2},{1,3},{2,0},{3,1},{4,6},{5,7},{6,4},{7,5},{8,10},{9,11},{10,... | collective-permute-start | bytes 552968 | tf_op jit(solution)/shard_map/ppermute | solution.py:235
  23.9 1.5 %collective-permute-done.4.from_z = bf16[144,640]{1,0:T(8,128)(2,1)S(1)} collective-permute-done((bf16[144,640]{1,0:T(8,128)(2,1)S(1)}, bf16[144,640]{1,0:T(8,128)(2,1)S(1)}, u32[]{:S(2)}, u32[]{:S(2)}) %collective-permute-start.4) | collective-permute-done | bytes 184352 | tf_op jit(solution)/shard_map/ppermute | solution.py:235
  25.4 1.4 %collective-permute-start.6 = (bf16[144,640]{1,0:T(8,128)(2,1)S(1)}, bf16[144,640]{1,0:T(8,128)(2,1)S(1)}, u32[]{:S(2)}, u32[]{:S(2)}) collective-permute-start(bf16[144,640]{1,0:T(8,128)(2,1)S(1)} %collective-permute-done.4.from_z), channel_id=1, source_target_pairs={{0,2},{1,3},{2,0},{3,1},{4,6},{5,7},{6,4},{7,5},{8,10},{9,11},{10,... | collective-permute-start | bytes 552968 | tf_op jit(solution)/shard_map/ppermute | solution.py:235
  27.1 2.1 %collective-permute-start.9 = (bf16[160,640]{1,0:T(8,128)(2,1)S(1)}, bf16[160,640]{1,0:T(8,128)(2,1)S(1)}, u32[]{:S(2)}, u32[]{:S(2)}) collective-permute-start(bf16[160,640]{1,0:T(8,128)(2,1)S(1)} %get-tuple-element.53.mine_0), channel_id=1, source_target_pairs={{0,16},{1,17},{2,18},{3,19},{4,20},{5,21},{6,22},{7,23},{8,24},{9,... | collective-permute-start | bytes 614408 | tf_op jit(solution)/shard_map/ppermute | solution.py:235
  29.2 1.6 %collective-permute-start.12 = (bf16[160,1024]{1,0:T(8,128)(2,1)S(1)}, bf16[160,1024]{1,0:T(8,128)(2,1)S(1)}, u32[]{:S(2)}, u32[]{:S(2)}) collective-permute-start(bf16[160,1024]{1,0:T(8,128)(2,1)S(1)} %get-tuple-element.61), channel_id=1, source_target_pairs={{0,8},{1,9},{2,10},{3,11},{4,12},{5,13},{6,14},{7,15},{8,0},{9,1},... | collective-permute-start | bytes 983048 | tf_op jit(solution)/shard_map/ppermute | solution.py:235
  32.6 3.8 %collective-permute-done.9.piece_2.mine_2 = bf16[160,640]{1,0:T(8,128)(2,1)S(1)} collective-permute-done((bf16[160,640]{1,0:T(8,128)(2,1)S(1)}, bf16[160,640]{1,0:T(8,128)(2,1)S(1)}, u32[]{:S(2)}, u32[]{:S(2)}) %collective-permute-start.9) | collective-permute-done | bytes 204832 | tf_op jit(solution)/shard_map/ppermute | solution.py:235
  37.7 1.5 %collective-permute-start.11 = (bf16[480,256]{1,0:T(8,128)(2,1)S(1)}, bf16[480,256]{1,0:T(8,128)(2,1)S(1)}, u32[]{:S(2)}, u32[]{:S(2)}) collective-permute-start(bf16[480,256]{1,0:T(8,128)(2,1)S(1)} %get-tuple-element.59), channel_id=1, source_target_pairs={{0,16},{1,17},{2,18},{3,19},{4,20},{5,21},{6,22},{7,23},{8,24},{9,... | collective-permute-start | bytes 737288 | tf_op jit(solution)/shard_map/ppermute | solution.py:235
  39.2 2.0 %collective-permute-done.12.kv_x0 = bf16[160,1024]{1,0:T(8,128)(2,1)S(1)} collective-permute-done((bf16[160,1024]{1,0:T(8,128)(2,1)S(1)}, bf16[160,1024]{1,0:T(8,128)(2,1)S(1)}, u32[]{:S(2)}, u32[]{:S(2)}) %collective-permute-start.12) | collective-permute-done | bytes 327712 | tf_op jit(solution)/shard_map/ppermute | solution.py:235
  41.7 4.9 %collective-permute-done.13.kv_x1.far_0 = bf16[160,1664]{1,0:T(8,128)(2,1)S(1)} collective-permute-done((bf16[160,1664]{1,0:T(8,128)(2,1)S(1)}, bf16[160,1664]{1,0:T(8,128)(2,1)S(1)}, u32[]{:S(2)}, u32[]{:S(2)}) %collective-permute-start.13) | collective-permute-done | bytes 532512 | tf_op jit(solution)/shard_map/ppermute | solution.py:235
  46.6 2.8 %collective-permute-done.11.received = bf16[480,256]{1,0:T(8,128)(2,1)S(1)} collective-permute-done((bf16[480,256]{1,0:T(8,128)(2,1)S(1)}, bf16[480,256]{1,0:T(8,128)(2,1)S(1)}, u32[]{:S(2)}, u32[]{:S(2)}) %collective-permute-start.11) | collective-permute-done | bytes 245792 | tf_op jit(solution)/shard_map/ppermute | solution.py:235
  49.6 2.4 %collective-permute-start.21 = (bf16[160,640]{1,0:T(8,128)(2,1)S(1)}, bf16[160,640]{1,0:T(8,128)(2,1)S(1)}, u32[]{:S(2)}, u32[]{:S(2)}) collective-permute-start(bf16[160,640]{1,0:T(8,128)(2,1)S(1)} %get-tuple-element.79), channel_id=1, source_target_pairs={{0,24},{1,25},{2,26},{3,27},{4,28},{5,29},{6,30},{7,31},{8,16},{9,... | collective-permute-start | bytes 614408 | tf_op jit(solution)/shard_map/ppermute | solution.py:235
  52.6 4.1 %shard_map.138 = (f32[80,1024]{1,0:T(8,128)S(1)}, f32[8,1024]{1,0:T(8,128)S(1)}, f32[8,1024]{1,0:T(8,128)S(1)}) custom-call(s32[2]{0:T(128)S(1)} %copy-done.4, s32[2]{0:T(128)S(1)} %copy-done.5, s32[2]{0:T(128)S(1)} %copy-done.6, bf16[80,1024]{1,0:T(8,128)(2,1)S(1)} %get-tuple-element.67.queries, bf16[160,1024]{1,0:T(8,128)(2,1)S(1)} %get-tuple-element.52.kv_own.kv_x0, ...), custom_call_target="tpu_custom_call" | custom-call | flops 1 | bytes 1 | tf_op jit(solution)/shard_map/pallas_call | solution.py:245
  56.7 4.0 %shard_map.139 = (f32[80,1024]{1,0:T(8,128)S(1)}, f32[8,1024]{1,0:T(8,128)S(1)}, f32[8,1024]{1,0:T(8,128)S(1)}) custom-call(s32[2]{0:T(128)S(1)} %copy-done.4, s32[2]{0:T(128)S(1)} %copy-done.5, s32[2]{0:T(128)S(1)} %copy-done.6, bf16[80,1024]{1,0:T(8,128)(2,1)S(1)} %get-tuple-element.67.queries, bf16[160,1024]{1,0:T(8,128)(2,1)S(1)} %collective-permute-done.12.kv_x0, ...), custom_call_target="tpu_custom_call" | custom-call | flops 1 | bytes 1 | tf_op jit(solution)/shard_map/pallas_call | solution.py:245
  60.9 1.5 %collective-permute-start.22 = (bf16[2,160,640]{2,1,0:T(8,128)(2,1)S(1)}, bf16[2,160,640]{2,1,0:T(8,128)(2,1)S(1)}, u32[]{:S(2)}, u32[]{:S(2)}) collective-permute-start(bf16[2,160,640]{2,1,0:T(8,128)(2,1)S(1)} %shard_map.141), channel_id=1, source_target_pairs={{0,4},{1,5},{2,6},{3,7},{4,0},{5,1},{6,2},{7,3},{8,12},{9,13},{10,... | collective-permute-start | bytes 1228808 | tf_op jit(solution)/shard_map/ppermute | solution.py:235
  63.5 1.6 %collective-permute-start.17 = (bf16[320,256]{1,0:T(8,128)(2,1)S(1)}, bf16[320,256]{1,0:T(8,128)(2,1)S(1)}, u32[]{:S(2)}, u32[]{:S(2)}) collective-permute-start(bf16[320,256]{1,0:T(8,128)(2,1)S(1)} %shard_map.140.own), channel_id=1, source_target_pairs={{0,2},{1,3},{2,0},{3,1},{4,6},{5,7},{6,4},{7,5},{8,10},{9,11},{10,... | collective-permute-start | bytes 491528 | tf_op jit(solution)/shard_map/ppermute | solution.py:235
  66.2 2.6 %collective-permute-done.17.from_y = bf16[320,256]{1,0:T(8,128)(2,1)S(1)} collective-permute-done((bf16[320,256]{1,0:T(8,128)(2,1)S(1)}, bf16[320,256]{1,0:T(8,128)(2,1)S(1)}, u32[]{:S(2)}, u32[]{:S(2)}) %collective-permute-start.17) | collective-permute-done | bytes 163872 | tf_op jit(solution)/shard_map/ppermute | solution.py:235
  68.9 1.9 %collective-permute-done.22 = bf16[2,160,640]{2,1,0:T(8,128)(2,1)S(1)} collective-permute-done((bf16[2,160,640]{2,1,0:T(8,128)(2,1)S(1)}, bf16[2,160,640]{2,1,0:T(8,128)(2,1)S(1)}, u32[]{:S(2)}, u32[]{:S(2)}) %collective-permute-start.22) | collective-permute-done | bytes 409632 | tf_op jit(solution)/shard_map/ppermute | solution.py:235
  74.3 2.0 %shard_map.144 = (bf16[160,1024]{1,0:T(8,128)(2,1)}, bf16[160,1024]{1,0:T(8,128)(2,1)}) custom-call(s32[2]{0:T(128)S(1)} %copy-done.5, s32[2]{0:T(128)S(1)} %copy-done.6, bf16[160,896]{1,0:T(8,128)(2,1)S(1)} %get-tuple-element.68.kv_mine, bf16[160,896]{1,0:T(8,128)(2,1)S(1)} %collective-permute-done.14.kv_other.far_2, ...), custom_call_target="tpu_custom_call" | custom-call | flops 1 | bytes 1 | tf_op jit(solution)/shard_map/pallas_call | solution.py:245
  76.3 2.1 %collective-permute-done.23 = bf16[128,640]{1,0:T(8,128)(2,1)S(1)} collective-permute-done((bf16[128,640]{1,0:T(8,128)(2,1)S(1)}, bf16[128,640]{1,0:T(8,128)(2,1)S(1)}, u32[]{:S(2)}, u32[]{:S(2)}) %collective-permute-start.23) | collective-permute-done | bytes 163872 | tf_op jit(solution)/shard_map/ppermute | solution.py:235
  (69 shorter events, 16.6 us)
Async XLA Ops:
  3.2 15.5 %collective-permute-start.3 = (bf16[320,480]{1,0:T(8,128)(2,1)}, bf16[320,480]{1,0:T(8,128)(2,1)S(1)}, u32[]{:S(2)}, u32[]{:S(2)}) collective-permute-start(bf16[320,480]{1,0:T(8,128)(2,1)} %get-tuple-element.46.near), channel_id=1, source_target_pairs={{0,4},{1,5},{2,6},{3,7},{4,0},{5,1},{6,2},{7,3},{8,12},{9,13},{10,... | collective-permute-start | bytes 921608 | tf_op jit(solution)/shard_map/ppermute | solution.py:235
  6.2 13.0 %collective-permute-start.2 = (bf16[320,480]{1,0:T(8,128)(2,1)}, bf16[320,480]{1,0:T(8,128)(2,1)S(1)}, u32[]{:S(2)}, u32[]{:S(2)}) collective-permute-start(bf16[320,480]{1,0:T(8,128)(2,1)} %get-tuple-element.45), channel_id=1, source_target_pairs={{0,8},{1,9},{2,10},{3,11},{4,12},{5,13},{6,14},{7,15},{8,0},{9,1},... | collective-permute-start | bytes 921608 | tf_op jit(solution)/shard_map/ppermute | solution.py:235
  7.7 10.9 %collective-permute-start = (bf16[128,640]{1,0:T(8,128)(2,1)}, bf16[128,640]{1,0:T(8,128)(2,1)S(1)}, u32[]{:S(2)}, u32[]{:S(2)}) collective-permute-start(bf16[128,640]{1,0:T(8,128)(2,1)} %tokens.3), channel_id=1, source_target_pairs={{2,16},{3,17},{6,20},{7,21},{10,24},{11,25},{14,28},{15,29},{16,2}... | collective-permute-start | bytes 491528 | tf_op jit(solution)/shard_map/ppermute | solution.py:235
  9.5 9.1 %collective-permute-start.1 = (f32[8,128]{1,0:T(8,128)S(1)}, f32[8,128]{1,0:T(8,128)S(1)}, u32[]{:S(2)}, u32[]{:S(2)}) collective-permute-start(f32[8,128]{1,0:T(8,128)S(1)} %get-tuple-element.44.squares), channel_id=1, source_target_pairs={{0,16},{1,17},{2,18},{3,19},{4,20},{5,21},{6,22},{7,23},{8,24},{9,... | collective-permute-start | bytes 12296 | tf_op jit(solution)/shard_map/ppermute | solution.py:235
  15.4 11.6 %collective-permute-start.8 = (bf16[160,640]{1,0:T(8,128)(2,1)}, bf16[160,640]{1,0:T(8,128)(2,1)S(1)}, u32[]{:S(2)}, u32[]{:S(2)}) collective-permute-start(bf16[160,640]{1,0:T(8,128)(2,1)} %slice.23), channel_id=1, source_target_pairs={{0,4},{1,5},{2,6},{3,7},{4,0},{5,1},{6,2},{7,3},{8,12},{9,13},{10,... | collective-permute-start | bytes 614408 | tf_op jit(solution)/shard_map/ppermute | solution.py:235
  19.2 6.2 %collective-permute-start.4 = (bf16[144,640]{1,0:T(8,128)(2,1)S(1)}, bf16[144,640]{1,0:T(8,128)(2,1)S(1)}, u32[]{:S(2)}, u32[]{:S(2)}) collective-permute-start(bf16[144,640]{1,0:T(8,128)(2,1)S(1)} %shard_map.131.current), channel_id=1, source_target_pairs={{0,8},{1,9},{2,10},{3,11},{4,12},{5,13},{6,14},{7,15},{8,0},{9,1},... | collective-permute-start | bytes 552968 | tf_op jit(solution)/shard_map/ppermute | solution.py:235
  21.9 8.9 %collective-permute-start.5 = (bf16[144,640]{1,0:T(8,128)(2,1)S(1)}, bf16[144,640]{1,0:T(8,128)(2,1)S(1)}, u32[]{:S(2)}, u32[]{:S(2)}) collective-permute-start(bf16[144,640]{1,0:T(8,128)(2,1)S(1)} %shard_map.131.current), channel_id=1, source_target_pairs={{0,2},{1,3},{2,0},{3,1},{4,6},{5,7},{6,4},{7,5},{8,10},{9,11},{10,... | collective-permute-start | bytes 552968 | tf_op jit(solution)/shard_map/ppermute | solution.py:235
  23.4 8.2 %collective-permute-start.10 = (bf16[320,480]{1,0:T(8,128)(2,1)S(1)}, bf16[320,480]{1,0:T(8,128)(2,1)S(1)}, u32[]{:S(2)}, u32[]{:S(2)}) collective-permute-start(bf16[320,480]{1,0:T(8,128)(2,1)S(1)} %collective-permute-done.2.near), channel_id=1, source_target_pairs={{0,4},{1,5},{2,6},{3,7},{4,0},{5,1},{6,2},{7,3},{8,12},{9,13},{10,... | collective-permute-start | bytes 921608 | tf_op jit(solution)/shard_map/ppermute | solution.py:235
  25.4 6.0 %collective-permute-start.6 = (bf16[144,640]{1,0:T(8,128)(2,1)S(1)}, bf16[144,640]{1,0:T(8,128)(2,1)S(1)}, u32[]{:S(2)}, u32[]{:S(2)}) collective-permute-start(bf16[144,640]{1,0:T(8,128)(2,1)S(1)} %collective-permute-done.4.from_z), channel_id=1, source_target_pairs={{0,2},{1,3},{2,0},{3,1},{4,6},{5,7},{6,4},{7,5},{8,10},{9,11},{10,... | collective-permute-start | bytes 552968 | tf_op jit(solution)/shard_map/ppermute | solution.py:235
  27.1 9.2 %collective-permute-start.9 = (bf16[160,640]{1,0:T(8,128)(2,1)S(1)}, bf16[160,640]{1,0:T(8,128)(2,1)S(1)}, u32[]{:S(2)}, u32[]{:S(2)}) collective-permute-start(bf16[160,640]{1,0:T(8,128)(2,1)S(1)} %get-tuple-element.53.mine_0), channel_id=1, source_target_pairs={{0,16},{1,17},{2,18},{3,19},{4,20},{5,21},{6,22},{7,23},{8,24},{9,... | collective-permute-start | bytes 614408 | tf_op jit(solution)/shard_map/ppermute | solution.py:235
  29.2 12.0 %collective-permute-start.12 = (bf16[160,1024]{1,0:T(8,128)(2,1)S(1)}, bf16[160,1024]{1,0:T(8,128)(2,1)S(1)}, u32[]{:S(2)}, u32[]{:S(2)}) collective-permute-start(bf16[160,1024]{1,0:T(8,128)(2,1)S(1)} %get-tuple-element.61), channel_id=1, source_target_pairs={{0,8},{1,9},{2,10},{3,11},{4,12},{5,13},{6,14},{7,15},{8,0},{9,1},... | collective-permute-start | bytes 983048 | tf_op jit(solution)/shard_map/ppermute | solution.py:235
  31.5 4.8 %collective-permute-start.7 = (bf16[4,144,640]{2,1,0:T(8,128)(2,1)S(1)}, bf16[4,144,640]{2,1,0:T(8,128)(2,1)S(1)}, u32[]{:S(2)}, u32[]{:S(2)}) collective-permute-start(bf16[4,144,640]{2,1,0:T(8,128)(2,1)S(1)} %pad_maximum_fusion), channel_id=1, source_target_pairs={{0,1},{1,0},{2,3},{3,2},{4,5},{5,4},{6,7},{7,6},{8,9},{9,8},{10,11... | collective-permute-start | bytes 2211848 | tf_op jit(solution)/shard_map/ppermute | solution.py:235
  31.7 15.0 %collective-permute-start.13 = (bf16[160,1664]{1,0:T(8,128)(2,1)S(1)}, bf16[160,1664]{1,0:T(8,128)(2,1)S(1)}, u32[]{:S(2)}, u32[]{:S(2)}) collective-permute-start(bf16[160,1664]{1,0:T(8,128)(2,1)S(1)} %get-tuple-element.63), channel_id=1, source_target_pairs={{0,4},{1,5},{2,6},{3,7},{4,0},{5,1},{6,2},{7,3},{8,12},{9,13},{10,... | collective-permute-start | bytes 1597448 | tf_op jit(solution)/shard_map/ppermute | solution.py:235
  37.7 11.7 %collective-permute-start.11 = (bf16[480,256]{1,0:T(8,128)(2,1)S(1)}, bf16[480,256]{1,0:T(8,128)(2,1)S(1)}, u32[]{:S(2)}, u32[]{:S(2)}) collective-permute-start(bf16[480,256]{1,0:T(8,128)(2,1)S(1)} %get-tuple-element.59), channel_id=1, source_target_pairs={{0,16},{1,17},{2,18},{3,19},{4,20},{5,21},{6,22},{7,23},{8,24},{9,... | collective-permute-start | bytes 737288 | tf_op jit(solution)/shard_map/ppermute | solution.py:235
  41.2 15.5 %collective-permute-start.15 = (bf16[160,1024]{1,0:T(8,128)(2,1)S(1)}, bf16[160,1024]{1,0:T(8,128)(2,1)S(1)}, u32[]{:S(2)}, u32[]{:S(2)}) collective-permute-start(bf16[160,1024]{1,0:T(8,128)(2,1)S(1)} %collective-permute-done.12.kv_x0), channel_id=1, source_target_pairs={{0,4},{1,5},{2,6},{3,7},{4,0},{5,1},{6,2},{7,3},{8,12},{9,13},{10,... | collective-permute-start | bytes 983048 | tf_op jit(solution)/shard_map/ppermute | solution.py:235
  49.6 11.2 %collective-permute-start.20 = (bf16[160,640]{1,0:T(8,128)(2,1)S(1)}, bf16[160,640]{1,0:T(8,128)(2,1)S(1)}, u32[]{:S(2)}, u32[]{:S(2)}) collective-permute-start(bf16[160,640]{1,0:T(8,128)(2,1)S(1)} %get-tuple-element.79), channel_id=1, source_target_pairs={{0,8},{1,9},{2,10},{3,11},{4,12},{5,13},{6,14},{7,15},{8,0},{9,1},... | collective-permute-start | bytes 614408 | tf_op jit(solution)/shard_map/ppermute | solution.py:235
  49.6 11.2 %collective-permute-start.21 = (bf16[160,640]{1,0:T(8,128)(2,1)S(1)}, bf16[160,640]{1,0:T(8,128)(2,1)S(1)}, u32[]{:S(2)}, u32[]{:S(2)}) collective-permute-start(bf16[160,640]{1,0:T(8,128)(2,1)S(1)} %get-tuple-element.79), channel_id=1, source_target_pairs={{0,24},{1,25},{2,26},{3,27},{4,28},{5,29},{6,30},{7,31},{8,16},{9,... | collective-permute-start | bytes 614408 | tf_op jit(solution)/shard_map/ppermute | solution.py:235
  52.1 10.3 %collective-permute-start.14 = (bf16[160,896]{1,0:T(8,128)(2,1)S(1)}, bf16[160,896]{1,0:T(8,128)(2,1)S(1)}, u32[]{:S(2)}, u32[]{:S(2)}) collective-permute-start(bf16[160,896]{1,0:T(8,128)(2,1)S(1)} %get-tuple-element.68.kv_mine), channel_id=1, source_target_pairs={{0,4},{1,5},{2,6},{3,7},{4,0},{5,1},{6,2},{7,3},{8,12},{9,13},{10,... | collective-permute-start | bytes 860168 | tf_op jit(solution)/shard_map/ppermute | solution.py:235
  60.9 9.9 %collective-permute-start.22 = (bf16[2,160,640]{2,1,0:T(8,128)(2,1)S(1)}, bf16[2,160,640]{2,1,0:T(8,128)(2,1)S(1)}, u32[]{:S(2)}, u32[]{:S(2)}) collective-permute-start(bf16[2,160,640]{2,1,0:T(8,128)(2,1)S(1)} %shard_map.141), channel_id=1, source_target_pairs={{0,4},{1,5},{2,6},{3,7},{4,0},{5,1},{6,2},{7,3},{8,12},{9,13},{10,... | collective-permute-start | bytes 1228808 | tf_op jit(solution)/shard_map/ppermute | solution.py:235
  63.5 5.4 %collective-permute-start.17 = (bf16[320,256]{1,0:T(8,128)(2,1)S(1)}, bf16[320,256]{1,0:T(8,128)(2,1)S(1)}, u32[]{:S(2)}, u32[]{:S(2)}) collective-permute-start(bf16[320,256]{1,0:T(8,128)(2,1)S(1)} %shard_map.140.own), channel_id=1, source_target_pairs={{0,2},{1,3},{2,0},{3,1},{4,6},{5,7},{6,4},{7,5},{8,10},{9,11},{10,... | collective-permute-start | bytes 491528 | tf_op jit(solution)/shard_map/ppermute | solution.py:235
  65.1 6.7 %collective-permute-start.16 = (bf16[320,256]{1,0:T(8,128)(2,1)S(1)}, bf16[320,256]{1,0:T(8,128)(2,1)S(1)}, u32[]{:S(2)}, u32[]{:S(2)}) collective-permute-start(bf16[320,256]{1,0:T(8,128)(2,1)S(1)} %shard_map.140.own), channel_id=1, source_target_pairs={{0,1},{1,0},{2,3},{3,2},{4,5},{5,4},{6,7},{7,6},{8,9},{9,8},{10,11... | collective-permute-start | bytes 491528 | tf_op jit(solution)/shard_map/ppermute | solution.py:235
  65.1 6.7 %collective-permute-start.19 = (bf16[2,160,256]{2,1,0:T(8,128)(2,1)S(1)}, bf16[2,160,256]{2,1,0:T(8,128)(2,1)S(1)}, u32[]{:S(2)}, u32[]{:S(2)}) collective-permute-start(bf16[2,160,256]{2,1,0:T(8,128)(2,1)S(1)} %pad_maximum_fusion.1), channel_id=1, source_target_pairs={{0,8},{1,9},{2,10},{3,11},{4,12},{5,13},{6,14},{7,15},{8,0},{9,1},... | collective-permute-start | bytes 491528 | tf_op jit(solution)/shard_map/ppermute | solution.py:235
  68.9 2.9 %collective-permute-start.18 = (bf16[320,256]{1,0:T(8,128)(2,1)S(1)}, bf16[320,256]{1,0:T(8,128)(2,1)S(1)}, u32[]{:S(2)}, u32[]{:S(2)}) collective-permute-start(bf16[320,256]{1,0:T(8,128)(2,1)S(1)} %collective-permute-done.17.from_y), channel_id=1, source_target_pairs={{0,1},{1,0},{2,3},{3,2},{4,5},{5,4},{6,7},{7,6},{8,9},{9,8},{10,11... | collective-permute-start | bytes 491528 | tf_op jit(solution)/shard_map/ppermute | solution.py:235
  72.5 5.9 %collective-permute-start.23 = (bf16[128,640]{1,0:T(8,128)(2,1)S(1)}, bf16[128,640]{1,0:T(8,128)(2,1)S(1)}, u32[]{:S(2)}, u32[]{:S(2)}) collective-permute-start(bf16[128,640]{1,0:T(8,128)(2,1)S(1)} %shard_map.143), channel_id=1, source_target_pairs={{0,8},{1,9},{2,10},{3,11},{4,12},{5,13},{6,14},{7,15},{8,0},{9,1},... | collective-permute-start | bytes 491528 | tf_op jit(solution)/shard_map/ppermute | solution.py:235
  (9 other events, 39.3 us)
